TPU v7x, 512 devices: a whole 4x8x8 slice. The times are simulated.
512 devices in a mesh: rep: 64 (over y, z_lo, core), fsdp: 8 (over x, z_hi).
Axes of the slice: x: 4, y: 8, z: 8 (z_hi: 2, z_lo: 4; z = z_hi * 4 + z_lo), core: 2. Of those that a mesh axis runs over, the one named last changes fastest.
Arguments:
- local_params: bfloat16 [64, 32, 14336], P('rep', 'fsdp'), may hold values from -1810 to 1810
- base: float32 [32, 14336], P('fsdp'), may hold values from -6 to 6
- momentum: float32 [32, 14336], P('fsdp'), may hold values from -4 to 4
Outputs:
- new_base: float32 [32, 14336], P('fsdp')
- new_momentum: float32 [32, 14336], P('fsdp')
All inputs are finite; a program needn't handle non-finite values.
Results may differ from a plain program's by a relative error of at most 0.006.
Values may be sent and summed in bfloat16 or wider, within the bound.
No kernel may reach another device: no remote copies, remote signals or barrier semaphores. Data moves between devices by JAX's collectives and lax.ppermute only.
A program may use at most 64 MiB of HBM per device.

v0:
```python
import math

import jax
import jax.numpy as jnp
from jax import lax
from jax.sharding import PartitionSpec as P

QBLOCK = 32


eps = 1e-06
clip_ratio = 0.2
outer_rate = 0.7
decay = 0.9
two_pi = 2.0 * math.pi


def staircase(values):
    return values - jnp.sin(two_pi * values) / two_pi


def quantize(values):
    count, length = values.shape
    blocks = values.reshape(count, length // QBLOCK, QBLOCK)
    top = jnp.max(jnp.abs(blocks), axis=-1)
    scale = ((top + eps) / 7.0).astype(jnp.bfloat16)
    code = staircase(blocks / scale.astype(jnp.float32)[..., None]).astype(jnp.bfloat16)
    return (code.reshape(count, length), scale)


def dequant(code, scale):
    count, length = code.shape
    blocks = code.reshape(count, length // QBLOCK, QBLOCK).astype(jnp.float32)
    return (blocks * scale.astype(jnp.float32)[..., None]).reshape(count, length)


def per_device(local_params, base, momentum):
    replicas = lax.axis_size("rep")
    shards = lax.axis_size("fsdp")
    rows, width = base.shape
    delta = base - local_params[0].astype(jnp.float32)
    pieces = delta.reshape(replicas, rows * width // replicas)
    code, scale = quantize(pieces)
    got_code, got_scale = (
        lax.all_to_all(code, "rep", split_axis=0, concat_axis=0, tiled=True),
        lax.all_to_all(scale, "rep", split_axis=0, concat_axis=0, tiled=True),
    )
    total = jnp.sum(dequant(got_code, got_scale), axis=0, keepdims=True)
    average = total / replicas
    code2, scale2 = quantize(average)
    owned = dequant(code2, scale2)
    squares = lax.psum(jnp.sum(owned * owned), ("rep", "fsdp"))
    all_code, all_scale = (
        lax.all_gather(code2, "rep", axis=0, tiled=True),
        lax.all_gather(scale2, "rep", axis=0, tiled=True),
    )
    grad = dequant(all_code, all_scale).reshape(rows, width)
    limit = clip_ratio * float(rows * width * shards) ** 0.5
    factor = limit / jnp.maximum(jnp.sqrt(squares), limit)
    scaled = factor * grad
    new_momentum = decay * momentum + scaled
    new_base = base - outer_rate * (scaled + decay * new_momentum)
    return (new_base, new_momentum)


def solution(mesh):
    return jax.shard_map(
        per_device,
        mesh=mesh,
        in_specs=(P("rep", "fsdp", None), P("fsdp", None), P("fsdp", None)),
        out_specs=(P("fsdp", None), P("fsdp", None)),
        check_vma=False,
    )
```

profile of v0, /device:TPU:1, one launch (start us, length us, event | category | flops | bytes accessed | tf_op | source)
XLA Modules:
  0.0 358.7 jit_solution(10810811767640576880)
XLA Ops:
  0.6 1.1 fusion.5
  1.7 0.4 abs.18
  2.2 0.3 reduce_max.18
  2.5 0.6 copy.17
  3.2 14.6 %all-to-all-start.1 = ((bf16[64,1,28]{2,1,0:T(2,128)(2,1)}), bf16[64,1,28]{2,1,0:T(2,128)(2,1)S(1)}, u32[]{:S(2)}, u32[]{:S(2)}) async-start(bf16[64,1,28]{2,1,0:T(2,128)(2,1)} %copy.17), calls=%async_computation.1 | async-start | bytes 65536 | tf_op jit(solution)/shard_map/all_to_all | solution.py:46
  17.8 0.1 copy.13
  17.9 0.2 copy.14
  18.1 0.1 reshape_reshape.4
  18.2 0.8 subtract_convert_fusion
  19.0 0.5 broadcast.240
  19.5 0.7 reduce.7
  20.2 0.8 reshape.290
  21.0 6.3 %all-to-all-done.1 = bf16[64,1,28]{2,1,0:T(2,128)(2,1)S(1)} async-done(((bf16[64,1,28]{2,1,0:T(2,128)(2,1)}), bf16[64,1,28]{2,1,0:T(2,128)(2,1)S(1)}, u32[]{:S(2)}, u32[]{:S(2)}) %all-to-all-start.1) | async-done | bytes 3616 | tf_op jit(solution)/shard_map/all_to_all | solution.py:46
  27.3 4.7 %all-to-all-start = ((bf16[64,2,448]{2,1,0:T(2,128)(2,1)}), bf16[64,2,448]{2,1,0:T(2,128)(2,1)S(1)}, u32[]{:S(2)}, u32[]{:S(2)}) async-start(bf16[64,2,448]{2,1,0:T(2,128)(2,1)} %reshape.290), calls=%async_computation | async-start | bytes 262144 | tf_op jit(solution)/shard_map/all_to_all | solution.py:45
  32.1 1.3 dynamic-slice
  33.4 0.1 copy.18
  33.5 9.7 %all-to-all-done = bf16[64,2,448]{2,1,0:T(2,128)(2,1)S(1)} async-done(((bf16[64,2,448]{2,1,0:T(2,128)(2,1)}), bf16[64,2,448]{2,1,0:T(2,128)(2,1)S(1)}, u32[]{:S(2)}, u32[]{:S(2)}) %all-to-all-start) | async-done | bytes 114720 | tf_op jit(solution)/shard_map/all_to_all | solution.py:45
  43.1 0.2 reshape.291
  43.4 0.2 copy.16
  43.6 0.2 fusion
  43.9 0.1 abs.20
  43.9 0.1 reduce_max.19
  44.1 0.1 div.89
  44.1 1.1 multiply_reduce_fusion
  45.9 98.5 %psum.7 = f32[]{:T(128)} all-reduce(f32[]{:T(128)} %multiply_reduce_fusion), channel_id=1, replica_groups=mesh['rep'=64,'fsdp'=8] {'rep','fsdp'}, use_global_device_ids=true, to_apply=%region_4.0 | all-reduce | flops 1 | bytes 8 | tf_op jit(solution)/shard_map/psum | solution.py:52
  145.2 0.1 div.96
  145.2 0.1 div.97
  145.3 0.1 convert_bitcast_fusion
  145.4 76.8 %all-gather.1 = bf16[64,1,896]{2,1,0:T(2,128)(2,1)S(1)} all-gather(bf16[1,1,896]{2,1,0:T(2,128)(2,1)S(1)} %convert_bitcast_fusion), channel_id=1, replica_groups=mesh['rep'=64,'fsdp'=8] {'rep'}, dimensions={0}, use_global_device_ids=true | all-gather | bytes 116480 | tf_op jit(solution)/shard_map/all_gather | solution.py:54
  222.2 0.6 convert_reduce_fusion
  222.9 0.1 reshape.277
  223.0 0.2 dynamic-update-slice
  223.2 133.1 %all-reduce = bf16[1792]{0:T(1024)(128)(2,1)S(1)} all-reduce(bf16[1792]{0:T(1024)(128)(2,1)S(1)} %dynamic-update-slice), channel_id=2, replica_groups=mesh['rep'=64,'fsdp'=8] {'rep'}, use_global_device_ids=true, to_apply=%add | all-reduce | flops 1792 | bytes 7168
  356.3 0.1 reshape.279
  356.4 0.3 mul.115
  356.7 0.0 copy-start
  356.8 0.0 copy-start.1
  356.8 0.4 mul.116
  357.2 0.5 copy-done
  357.7 0.1 copy-done.1
  357.8 0.9 multiply_subtract_fusion
  (7 shorter events, 0.1 us)
Async XLA Ops:
  3.2 24.2 %all-to-all-start.1 = ((bf16[64,1,28]{2,1,0:T(2,128)(2,1)}), bf16[64,1,28]{2,1,0:T(2,128)(2,1)S(1)}, u32[]{:S(2)}, u32[]{:S(2)}) async-start(bf16[64,1,28]{2,1,0:T(2,128)(2,1)} %copy.17), calls=%async_computation.1 | async-start | bytes 65536 | tf_op jit(solution)/shard_map/all_to_all | solution.py:46
  27.3 15.8 %all-to-all-start = ((bf16[64,2,448]{2,1,0:T(2,128)(2,1)}), bf16[64,2,448]{2,1,0:T(2,128)(2,1)S(1)}, u32[]{:S(2)}, u32[]{:S(2)}) async-start(bf16[64,2,448]{2,1,0:T(2,128)(2,1)} %reshape.290), calls=%async_computation | async-start | bytes 262144 | tf_op jit(solution)/shard_map/all_to_all | solution.py:45
  356.7 0.9 copy-start
  356.8 1.0 copy-start.1
where the time goes:
time: 359 us
  blocking collectives  308 us (86%)
  starting transfers between devices  19.3 us (5%)
  waiting for transfers between devices  16 us (4%)
  local copies, waits for them, and re-layouts  6.77 us (2%)
  other arithmetic  6.09 us (2%)
    unnamed x1, blocking collectives  133 us
    psum x1, blocking collectives, per_device(): squares = lax.psum(jnp.sum(owned * owned), ('rep', 'fsdp'))  98.5 us
    all_gather x1, blocking collectives, per_device(): lax.all_gather(code2, 'rep', axis=0, tiled=True)  76.8 us
    all_to_all x1, starting transfers between devices, per_device(): lax.all_to_all(scale, 'rep', split_axis=0, concat_axis=0, tiled=True)  14.6 us
    all_to_all x1, waiting for transfers between devices, per_device(): lax.all_to_all(code, 'rep', split_axis=0, concat_axis=0, tiled=True)  9.67 us
  transfers between devices with their start and end apart: 2, of which 2 were waited for; matrix products, arithmetic and copies ran while one was open for 1% of the time, Pallas kernels for 0%

commit v1 on v0

--- a/solution.py
+++ b/solution.py
@@ -41,20 +41,25 @@
     delta = base - local_params[0].astype(jnp.float32)
     pieces = delta.reshape(replicas, rows * width // replicas)
     code, scale = quantize(pieces)
-    got_code, got_scale = (
-        lax.all_to_all(code, "rep", split_axis=0, concat_axis=0, tiled=True),
-        lax.all_to_all(scale, "rep", split_axis=0, concat_axis=0, tiled=True),
+    got = lax.all_to_all(
+        jnp.concatenate([code, scale], axis=1), "rep", split_axis=0, concat_axis=0, tiled=True
     )
+    got_code, got_scale = got[:, : code.shape[1]], got[:, code.shape[1] :]
     total = jnp.sum(dequant(got_code, got_scale), axis=0, keepdims=True)
     average = total / replicas
     code2, scale2 = quantize(average)
     owned = dequant(code2, scale2)
-    squares = lax.psum(jnp.sum(owned * owned), ("rep", "fsdp"))
-    all_code, all_scale = (
-        lax.all_gather(code2, "rep", axis=0, tiled=True),
-        lax.all_gather(scale2, "rep", axis=0, tiled=True),
+    message = jnp.concatenate([code2, scale2], axis=1)
+    spread = lax.all_to_all(
+        jnp.broadcast_to(message, (replicas, message.shape[1])), "rep", split_axis=0, concat_axis=0, tiled=True
     )
-    grad = dequant(all_code, all_scale).reshape(rows, width)
+    all_code, all_scale = spread[:, : code2.shape[1]], spread[:, code2.shape[1] :]
+    owned = dequant(all_code, all_scale)
+    part = jnp.sum(owned * owned)
+    squares = jnp.sum(
+        lax.all_to_all(jnp.broadcast_to(part, (shards, 1, 128)), "fsdp", split_axis=0, concat_axis=0, tiled=True)[:, 0, 0]
+    )
+    grad = owned.reshape(rows, width)
     limit = clip_ratio * float(rows * width * shards) ** 0.5
     factor = limit / jnp.maximum(jnp.sqrt(squares), limit)
     scaled = factor * grad

time: 359 us -> 71.7 us (0.20)
  blocking collectives: 308 us -> 40 us
  starting transfers between devices: 19.3 us -> 9.77 us
  waiting for transfers between devices: 16 us -> 7.62 us
    unnamed x1 -> x0, blocking collectives: 133 us -> none
    psum x1 -> x0, blocking collectives: 98.5 us -> none  [per_device(): squares = lax.psum(jnp.sum(owned * owned), ('rep', 'fsdp'))]
    all_gather x1 -> x0, blocking collectives: 76.8 us -> none  [per_device(): lax.all_gather(code2, 'rep', axis=0, tiled=True)]
    all_to_all x0 -> x2, blocking collectives: none -> 40 us  [the longest x1 25.3 us: per_device(): lax.all_to_all(jnp.concatenate([code, scale], axis=1), 'rep', split_axis=...]
    all_to_all x2 -> x1, starting transfers between devices: 19.3 us -> 9.77 us  [per_device(): lax.all_to_all(jnp.broadcast_to(part, (shards, 1, 128)), 'fsdp', split_ax...]
    all_to_all x2 -> x1, waiting for transfers between devices: 16 us -> 7.62 us  [per_device(): lax.all_to_all(jnp.broadcast_to(part, (shards, 1, 128)), 'fsdp', split_ax...]
  transfers between devices with their start and end apart: 2 -> 1, of which waited for: 2 -> 1; matrix products, arithmetic and copies ran while one was open for 1% -> 2% of each run, Pallas kernels for 0% -> 0%
where the time goes in v1:
time: 71.7 us; the launch traced here: 71.5 us
  blocking collectives  40 us (56%)
  starting transfers between devices  9.77 us (14%)
  waiting for transfers between devices  7.62 us (11%)
  other arithmetic  7.19 us (10%)
  local copies, waits for them, and re-layouts  5.29 us (7%)
  between operations  1.56 us (2%)
    all_to_all x1, blocking collectives, per_device(): lax.all_to_all(jnp.concatenate([code, scale], axis=1), 'rep', split_axis=...  25.3 us
    all_to_all x1, blocking collectives, per_device(): lax.all_to_all(jnp.broadcast_to(message, (replicas, message.shape[1])), '...  14.7 us
    all_to_all x1, starting transfers between devices, per_device(): lax.all_to_all(jnp.broadcast_to(part, (shards, 1, 128)), 'fsdp', split_ax...  9.77 us
    all_to_all x1, waiting for transfers between devices, per_device(): lax.all_to_all(jnp.broadcast_to(part, (shards, 1, 128)), 'fsdp', split_ax...  7.62 us
  transfers between devices with their start and end apart: 1, of which 1 were waited for; matrix products, arithmetic and copies ran while one was open for 2% of the time, Pallas kernels for 0%

profile of v1, /device:TPU:1, one launch (start us, length us, event | category | flops | bytes accessed | tf_op | source)
XLA Modules:
  0.0 71.5 jit_solution(13929421994713693271)
XLA Ops:
  0.6 1.1 %fusion.4 = (f32[4,14336]{1,0:T(4,128)S(1)}, f32[4,14336]{1,0:T(4,128)S(1)}) fusion(f32[4,14336]{1,0:T(4,128)} %param.4, bf16[1,4,14336]{2,1,0:T(4,128)(2,1)} %param.3), kind=kLoop, calls=%fused_computation.24 | loop fusion | flops 172032 | bytes 802816 | tf_op jit(solution)/shard_map/abs | solution.py:25
  1.7 0.1 reshape_reshape.4
  1.9 0.4 abs.21
  2.3 0.3 reduce_max.18
  2.7 0.1 copy.48
  2.7 0.1 copy.50
  2.9 0.2 copy.49
  3.1 0.8 %subtract_convert_fusion = bf16[64,896]{1,0:T(8,128)(2,1)S(1)} fusion(f32[64,896]{1,0:T(8,128)S(1)} %reshape_reshape.4, f32[64,896]{1,0:T(8,128)S(1)} %copy.49), kind=kLoop, calls=%fused_computation.10 | loop fusion | flops 286720 | bytes 573440 | tf_op jit(solution)/shard_map/convert_element_type | solution.py:27
  3.9 0.5 broadcast.147
  4.4 0.7 reduce.5
  5.1 0.2 reshape.145
  5.3 25.3 %all_to_all.26 = bf16[64,2,462]{2,1,0:T(2,128)(2,1)S(1)} all-to-all(bf16[64,2,462]{2,1,0:T(2,128)(2,1)S(1)} %reshape.145), channel_id=1, replica_groups=mesh['rep'=64,'fsdp'=8] {'rep'}, dimensions={0} | all-to-all | bytes 236544 | tf_op jit(solution)/shard_map/all_to_all | solution.py:44
  30.6 0.2 reshape.146
  30.8 0.2 copy.52
  31.0 0.2 fusion.2
  31.2 0.1 abs.23
  31.3 0.1 reduce_max.19
  31.4 0.1 div.66
  31.5 0.1 div.67
  31.6 0.1 subtract_convert_fusion.1
  31.7 0.1 broadcast_in_dim.4
  31.9 1.4 %reduce.6 = bf16[64,924]{1,0:T(8,128)(2,1)S(1)} reduce(bf16[64,1,924]{2,1,0:T(2,128)(2,1)S(1)} %broadcast_in_dim.4, bf16[]{:T(256)} %broadcast.147), dimensions={1}, to_apply=%broadcast_in_dim.4.reduce_sub_computation | reduce | bytes 236546 | tf_op jit(solution)/shard_map/broadcast_in_dim | solution.py:54
  33.3 0.2 reshape.147
  33.5 14.7 %all_to_all.27 = bf16[64,2,462]{2,1,0:T(2,128)(2,1)S(1)} all-to-all(bf16[64,2,462]{2,1,0:T(2,128)(2,1)S(1)} %reshape.147), channel_id=1, replica_groups=mesh['rep'=64,'fsdp'=8] {'rep'}, dimensions={0} | all-to-all | bytes 236544 | tf_op jit(solution)/shard_map/all_to_all | solution.py:53
  48.2 0.2 reshape.148
  48.4 0.2 copy.53
  48.6 0.7 %fusion.1 = f32[]{:T(128)} fusion(f32[64,28]{0,1:T(8,128)S(1)} %slice_convert_fusion.1, bf16[64,924]{0,1:T(8,128)(2,1)S(1)} %bitcast.24), kind=kLoop, calls=%fused_computation.2 | loop fusion | flops 229375 | bytes 121860 | tf_op jit(solution)/shard_map/reduce_sum | solution.py:58
  49.3 1.2 %broadcast_in_dim.5 = f32[8,1,128]{2,1,0:T(1,128)} broadcast(f32[]{:T(128)} %fusion.1), dimensions={} | broadcast | bytes 4100 | tf_op jit(solution)/shard_map/broadcast_in_dim | solution.py:60
  50.5 9.8 %all-to-all-start.2 = ((f32[8,1,128]{2,1,0:T(1,128)}), f32[8,1,128]{2,1,0:T(1,128)S(1)}, u32[]{:S(2)}, u32[]{:S(2)}) async-start(f32[8,1,128]{2,1,0:T(1,128)} %broadcast_in_dim.5), calls=%async_computation.2 | async-start | bytes 8192 | tf_op jit(solution)/shard_map/all_to_all | solution.py:60
  60.3 0.1 copy.54
  60.4 0.2 copy.57
  60.6 0.1 reshape.143
  60.7 0.3 mul.69
  61.1 0.0 copy-start
  61.1 0.0 copy-start.1
  61.1 0.4 mul.74
  61.5 7.6 %all-to-all-done.2 = f32[8,1,128]{2,1,0:T(1,128)S(1)} async-done(((f32[8,1,128]{2,1,0:T(1,128)}), f32[8,1,128]{2,1,0:T(1,128)S(1)}, u32[]{:S(2)}, u32[]{:S(2)}) %all-to-all-start.2) | async-done | bytes 4128 | tf_op jit(solution)/shard_map/all_to_all | solution.py:60
  69.1 0.6 slice_reduce_fusion
  70.5 0.0 copy-done
  70.5 0.0 copy-done.1
  70.5 0.9 %multiply_subtract_fusion = (f32[4,14336]{1,0:T(4,128)}, f32[4,14336]{1,0:T(4,128)}) fusion(f32[4,14336]{1,0:T(4,128)S(1)} %copy-done, f32[4,14336]{1,0:T(4,128)S(1)} %reshape.143, f32[4,14336]{1,0:T(4,128)S(1)} %mul.74, f32[]{:T(128)S(6)} %div.70, f32[4,14336]{1,0:T(4,128)S(1)} %copy-done.1), kind=kLoop, calls=%fused_computation.7 | loop fusion | flops 458752 | bytes 1376260 | tf_op jit(solution)/shard_map/sub | solution.py:67
  (9 shorter events, 0.1 us)
Async XLA Ops:
  50.5 18.6 %all-to-all-start.2 = ((f32[8,1,128]{2,1,0:T(1,128)}), f32[8,1,128]{2,1,0:T(1,128)S(1)}, u32[]{:S(2)}, u32[]{:S(2)}) async-start(f32[8,1,128]{2,1,0:T(1,128)} %broadcast_in_dim.5), calls=%async_computation.2 | async-start | bytes 8192 | tf_op jit(solution)/shard_map/all_to_all | solution.py:60
  61.1 9.4 %copy-start = (f32[4,14336]{1,0:T(4,128)S(1)}, f32[4,14336]{1,0:T(4,128)}, u32[]{:S(2)}) copy-start(f32[4,14336]{1,0:T(4,128)} %param.4) | copy-start | bytes 688132
  61.1 9.4 %copy-start.1 = (f32[4,14336]{1,0:T(4,128)S(1)}, f32[4,14336]{1,0:T(4,128)}, u32[]{:S(2)}) copy-start(f32[4,14336]{1,0:T(4,128)} %param.5) | copy-start | bytes 688132

commit v2 on v0

v2 whole, which is shorter than its diff:
```python
import math

import jax
import jax.numpy as jnp
from jax import lax
from jax.experimental import pallas as pl
from jax.experimental.pallas import tpu as pltpu
from jax.sharding import PartitionSpec as P

QBLOCK = 32
LANES = 128
UNIT = 8

eps = 1e-06
clip_ratio = 0.2
outer_rate = 0.7
decay = 0.9

STAIR = (6.57973575592041, -12.987854957580566, 12.20757007598877, -6.687924861907959, 2.368926763534546, -0.5121700763702393)


def staircase(values):
    near = jnp.round(values)
    rest = values - near
    square = rest * rest
    poly = jnp.full_like(square, STAIR[-1])
    for coefficient in STAIR[-2::-1]:
        poly = poly * square + coefficient
    return near + rest * square * poly


def rows_of(shape):
    return lax.broadcasted_iota(jnp.int32, shape, 0) % UNIT


def lanes_of(shape):
    return lax.broadcasted_iota(jnp.int32, shape, 1) % QBLOCK


def block_ones():
    one = lax.broadcasted_iota(jnp.int32, (LANES, LANES), 0) // QBLOCK
    two = lax.broadcasted_iota(jnp.int32, (LANES, LANES), 1) // QBLOCK
    return jnp.where(one == two, 1.0, 0.0).astype(jnp.bfloat16)


def spread(values, ones):
    return jnp.dot(values.astype(jnp.bfloat16), ones, preferred_element_type=jnp.float32)


def encode(values, ones):
    shape = values.shape
    row, lane = rows_of(shape), lanes_of(shape)
    values = jnp.where(row < UNIT - 1, values, 0.0)
    top = jnp.abs(values)
    for shift in (1, 2, 4, 8, 16):
        top = jnp.maximum(top, pltpu.roll(top, shift, 1))
    scale = jnp.where(lane == QBLOCK - 1, (top + eps) * (1.0 / 7.0), 0.0)
    scale = spread(scale, ones)
    code = staircase(values / scale)
    own = jnp.where((lane == row) & (row < UNIT - 1), scale, 0.0)
    groups = (shape[0] // UNIT, UNIT, LANES)
    line = jnp.sum(own.reshape(groups), axis=1, keepdims=True)
    line = jnp.broadcast_to(line, groups).reshape(shape)
    return jnp.where(row == UNIT - 1, line, code).astype(jnp.bfloat16)


def decode(message, ones):
    shape = message.shape
    row, lane = rows_of(shape), lanes_of(shape)
    message = message.astype(jnp.float32)
    groups = (shape[0] // UNIT, UNIT, LANES)
    line = message.reshape(groups)[:, UNIT - 1 :, :]
    line = jnp.broadcast_to(line, groups).reshape(shape)
    own = jnp.where((lane == row) & (row < UNIT - 1), line, 0.0)
    return message * spread(own, ones)


def first_kernel(local_ref, base_ref, out_ref, delta_ref):
    ones = block_ones()
    rows = base_ref.shape[0]
    chunk = UNIT * UNIT
    step = rows // UNIT
    delta_ref[:rows] = base_ref[...] - local_ref[...].astype(jnp.float32)
    for a in range(UNIT):
        pieces = [delta_ref[pl.ds(a * step + s, UNIT, stride=UNIT)] for s in range(UNIT)]
        out_ref[a * chunk : (a + 1) * chunk] = encode(jnp.concatenate(pieces, axis=0), ones)


def second_kernel(in_ref, out_ref, *, replicas):
    ones = block_ones()
    chunk = UNIT * UNIT
    total = jnp.zeros((UNIT, LANES), jnp.float32)
    for a in range(UNIT):
        values = decode(in_ref[a * chunk : (a + 1) * chunk], ones)
        total += jnp.sum(values.reshape(UNIT, UNIT, LANES), axis=0)
    message = encode(total / replicas, ones)
    message = jnp.concatenate([message.astype(jnp.float32)] * UNIT, axis=0).astype(jnp.bfloat16)
    for a in range(UNIT):
        out_ref[a * chunk : (a + 1) * chunk] = message


def third_kernel(in_ref, grad_ref, squares_ref):
    ones = block_ones()
    chunk = UNIT * UNIT
    step = grad_ref.shape[0] // UNIT
    total = jnp.zeros((UNIT, LANES), jnp.float32)
    for a in range(UNIT):
        values = decode(in_ref[a * chunk : (a + 1) * chunk], ones)
        total += jnp.sum((values * values).reshape(UNIT, UNIT, LANES), axis=0)
        for s in range(UNIT):
            grad_ref[pl.ds(a * step + s, UNIT - 1, stride=UNIT)] = values[s * UNIT : s * UNIT + UNIT - 1]
    squares_ref[...] = jnp.full((UNIT, LANES), jnp.sum(total), jnp.float32)


def fourth_kernel(grad_ref, base_ref, momentum_ref, squares_ref, new_base_ref, new_momentum_ref, *, limit):
    squares = jnp.sum(squares_ref[...], axis=0, keepdims=True)
    factor = limit / jnp.maximum(jnp.sqrt(squares), limit)
    scaled = factor * grad_ref[...]
    momentum = decay * momentum_ref[...] + scaled
    new_momentum_ref[...] = momentum
    new_base_ref[...] = base_ref[...] - outer_rate * (scaled + decay * momentum)


def to_units(array):
    rows, width = array.shape
    return array.reshape(rows, width // LANES, LANES).transpose(1, 0, 2).reshape(rows * width // LANES, LANES)


def from_units(array, rows, width):
    return array.reshape(width // LANES, rows, LANES).transpose(1, 0, 2).reshape(rows, width)


def per_device(groups, local_params, base, momentum):
    replicas = lax.axis_size("rep")
    shards = lax.axis_size("fsdp")
    rows, width = base.shape
    units = rows * width // LANES
    f32 = jnp.float32
    message = jax.ShapeDtypeStruct((replicas * UNIT, LANES), jnp.bfloat16)

    def exchange(array):
        array = array.reshape(replicas, UNIT, LANES)
        return lax.all_to_all(array, "rep", split_axis=0, concat_axis=0, tiled=True).reshape(message.shape)

    base_units = to_units(base)
    pieces = pl.pallas_call(
        first_kernel,
        out_shape=message,
        scratch_shapes=[pltpu.VMEM((units + UNIT * UNIT, LANES), f32)],
    )(to_units(local_params[0]), base_units)
    owned = pl.pallas_call(
        lambda *refs: second_kernel(*refs, replicas=replicas),
        out_shape=message,
    )(exchange(pieces))
    grad, squares = pl.pallas_call(
        third_kernel,
        out_shape=(jax.ShapeDtypeStruct((units, LANES), f32), jax.ShapeDtypeStruct((shards, LANES), f32)),
    )(exchange(owned))
    squares = lax.all_to_all(
        squares.reshape(shards, 1, LANES), ("rep", "fsdp"), split_axis=0, concat_axis=0, tiled=True, axis_index_groups=groups
    ).reshape(shards, LANES)
    limit = clip_ratio * float(rows * width * shards) ** 0.5
    new_base, new_momentum = pl.pallas_call(
        lambda *refs: fourth_kernel(*refs, limit=limit),
        out_shape=(jax.ShapeDtypeStruct((units, LANES), f32),) * 2,
    )(grad, base_units, to_units(momentum), squares)
    return from_units(new_base, rows, width), from_units(new_momentum, rows, width)


def near_groups(mesh):
    replicas, shards = mesh.shape["rep"], mesh.shape["fsdp"]

    def index(y, z, core, x):
        return ((y * 4 + z % 4) * 2 + core) * shards + x * 2 + z // 4

    partner = {0: 6, 1: 7, 2: 4, 3: 5}
    return [
        [index(y, z, core, x) for x in range(shards // 2) for z in (low, partner[low])]
        for y in range(replicas // 8)
        for low in range(4)
        for core in range(2)
    ]


def solution(mesh):
    groups = near_groups(mesh)
    return jax.shard_map(
        lambda *arrays: per_device(groups, *arrays),
        mesh=mesh,
        in_specs=(P("rep", "fsdp", None), P("fsdp", None), P("fsdp", None)),
        out_specs=(P("fsdp", None), P("fsdp", None)),
        check_vma=False,
    )
```

time: 359 us -> 67.1 us (0.19)
  blocking collectives: 308 us -> 57.7 us
  starting transfers between devices: 19.3 us -> 0 us
  waiting for transfers between devices: 16 us -> 0 us
  Pallas kernels: 0 us -> 8.5 us
  local copies, waits for them, and re-layouts: 6.77 us -> 0 us
  other arithmetic: 6.09 us -> 0 us
    unnamed x1 -> x0, blocking collectives: 133 us -> none
    psum x1 -> x0, blocking collectives: 98.5 us -> none  [per_device(): squares = lax.psum(jnp.sum(owned * owned), ('rep', 'fsdp'))]
    all_gather x1 -> x0, blocking collectives: 76.8 us -> none  [per_device(): lax.all_gather(code2, 'rep', axis=0, tiled=True)]
    all_to_all x0 -> x3, blocking collectives: none -> 57.7 us  [the longest x2 41.9 us: exchange(): lax.all_to_all(array, 'rep', split_axis=0, concat_axis=0, tiled=True)]
    all_to_all x2 -> x0, starting transfers between devices: 19.3 us -> none  [the longest x1 14.6 us: per_device(): lax.all_to_all(scale, 'rep', split_axis=0, concat_axis=0, tiled=True)]
    all_to_all x2 -> x0, waiting for transfers between devices: 16 us -> none  [the longest x1 9.67 us: per_device(): lax.all_to_all(code, 'rep', split_axis=0, concat_axis=0, tiled=True)]
    pallas_call x0 -> x4, Pallas kernels: none -> 8.5 us  [the longest x1 2.41 us: per_device(): pl.pallas_call(first_kernel, out_shape=message, scratch_shapes=[pltpu.VME...]
  transfers between devices with their start and end apart: 2 -> 0, of which waited for: 2 -> 0; matrix products, arithmetic and copies ran while one was open for 1% -> 0% of each run, Pallas kernels for 0% -> 0%
where the time goes in v2:
time: 67.1 us; the launch traced here: 66.8 us
  blocking collectives  57.7 us (86%)
  Pallas kernels  8.5 us (13%)
    all_to_all x2, blocking collectives, exchange(): lax.all_to_all(array, 'rep', split_axis=0, concat_axis=0, tiled=True)  41.9 us
    all_to_all x1, blocking collectives, per_device(): lax.all_to_all(squares.reshape(shards, 1, LANES), ('rep', 'fsdp'), split_...  15.8 us
    pallas_call x1, Pallas kernels, per_device(): pl.pallas_call(first_kernel, out_shape=message, scratch_shapes=[pltpu.VME...  2.41 us
    pallas_call x1, Pallas kernels, per_device(): pl.pallas_call(lambda *refs: second_kernel(*refs, replicas=replicas), out...  2.27 us
    pallas_call x1, Pallas kernels, per_device(): pl.pallas_call(lambda *refs: fourth_kernel(*refs, limit=limit), out_shape...  1.98 us
    pallas_call x1, Pallas kernels, per_device(): pl.pallas_call(third_kernel, out_shape=(jax.ShapeDtypeStruct((units, LANE...  1.83 us

profile of v2, /device:TPU:1, one launch (start us, length us, event | category | flops | bytes accessed | tf_op | source)
XLA Modules:
  0.0 66.8 jit_solution(17319389902939952229)
XLA Ops:
  0.6 2.4 %shard_map.50 = bf16[512,128]{1,0:T(8,128)(2,1)} custom-call(bf16[448,128]{1,0:T(8,128)(2,1)} %bitcast.40, f32[448,128]{1,0:T(8,128)} %bitcast.33), custom_call_target="tpu_custom_call" | custom-call | tf_op jit(solution)/shard_map/pallas_call | solution.py:146
  3.0 25.6 %all_to_all.15 = bf16[64,8,128]{2,1,0:T(8,128)(2,1)} all-to-all(bf16[64,8,128]{2,1,0:T(8,128)(2,1)} %bitcast.38), channel_id=1, replica_groups=mesh['rep'=64,'fsdp'=8] {'rep'}, dimensions={0} | all-to-all | bytes 262144 | tf_op jit(solution)/shard_map/all_to_all | solution.py:143
  28.7 2.3 %shard_map.51 = bf16[512,128]{1,0:T(8,128)(2,1)} custom-call(bf16[512,128]{1,0:T(8,128)(2,1)} %bitcast.36), custom_call_target="tpu_custom_call" | custom-call | tf_op jit(solution)/shard_map/pallas_call | solution.py:151
  30.9 16.2 %all_to_all.16 = bf16[64,8,128]{2,1,0:T(8,128)(2,1)} all-to-all(bf16[64,8,128]{2,1,0:T(8,128)(2,1)} %bitcast.37), channel_id=1, replica_groups=mesh['rep'=64,'fsdp'=8] {'rep'}, dimensions={0} | all-to-all | bytes 262144 | tf_op jit(solution)/shard_map/all_to_all | solution.py:143
  47.2 1.8 %shard_map.52 = (f32[448,128]{1,0:T(8,128)}, f32[8,128]{1,0:T(8,128)}) custom-call(bf16[512,128]{1,0:T(8,128)(2,1)} %bitcast.35), custom_call_target="tpu_custom_call" | custom-call | tf_op jit(solution)/shard_map/pallas_call | solution.py:155
  49.0 15.8 %all_to_all.17 = f32[8,1,128]{2,1,0:T(1,128)} all-to-all(f32[8,1,128]{2,1,0:T(1,128)} %bitcast.42), channel_id=1, replica_groups={{0,33,2,35,4,37,6,39},{8,41,10,43,12,45,14,47},{16,49,18,51,20,53,22,55..., dimensions={0} | all-to-all | bytes 8192 | tf_op jit(solution)/shard_map/all_to_all | solution.py:159
  64.8 2.0 %shard_map.53 = (f32[448,128]{1,0:T(8,128)}, f32[448,128]{1,0:T(8,128)}) custom-call(f32[448,128]{1,0:T(8,128)} %get-tuple-element.6.refs_0_, f32[448,128]{1,0:T(8,128)} %bitcast.34, f32[448,128]{1,0:T(8,128)} %bitcast.39, f32[8,128]{1,0:T(8,128)} %bitcast.41), custom_call_target="tpu_custom_call" | custom-call | tf_op jit(solution)/shard_map/pallas_call | solution.py:163

commit v3 on v2

--- a/solution.py
+++ b/solution.py
@@ -10,6 +10,7 @@
 QBLOCK = 32
 LANES = 128
 UNIT = 8
+PARAMS = pltpu.CompilerParams(vmem_limit_bytes=4 << 20)
 
 eps = 1e-06
 clip_ratio = 0.2
@@ -145,15 +146,18 @@
     base_units = to_units(base)
     pieces = pl.pallas_call(
         first_kernel,
+        compiler_params=PARAMS,
         out_shape=message,
         scratch_shapes=[pltpu.VMEM((units + UNIT * UNIT, LANES), f32)],
     )(to_units(local_params[0]), base_units)
     owned = pl.pallas_call(
         lambda *refs: second_kernel(*refs, replicas=replicas),
+        compiler_params=PARAMS,
         out_shape=message,
     )(exchange(pieces))
     grad, squares = pl.pallas_call(
         third_kernel,
+        compiler_params=PARAMS,
         out_shape=(jax.ShapeDtypeStruct((units, LANES), f32), jax.ShapeDtypeStruct((shards, LANES), f32)),
     )(exchange(owned))
     squares = lax.all_to_all(
@@ -162,6 +166,7 @@
     limit = clip_ratio * float(rows * width * shards) ** 0.5
     new_base, new_momentum = pl.pallas_call(
         lambda *refs: fourth_kernel(*refs, limit=limit),
+        compiler_params=PARAMS,
         out_shape=(jax.ShapeDtypeStruct((units, LANES), f32),) * 2,
     )(grad, base_units, to_units(momentum), squares)
     return from_units(new_base, rows, width), from_units(new_momentum, rows, width)

time: 67.1 us -> 61.2 us (0.912)
  Pallas kernels: 8.5 us -> 2.6 us
  blocking collectives: 57.7 us -> 55.8 us
  local copies, waits for them, and re-layouts: 0 us -> 1.84 us
    pallas_call x4, Pallas kernels: 8.5 us -> 2.6 us  [the longest x1 0.83 us: per_device(): pl.pallas_call(lambda *refs: fourth_kernel(*refs, limit=limit), compiler_...]
    unnamed x0 -> x8, local copies, waits for them, and re-layouts: none -> 1.84 us
    all_to_all x2, blocking collectives: 41.9 us -> 40.2 us  [exchange(): lax.all_to_all(array, 'rep', split_axis=0, concat_axis=0, tiled=True)]
where the time goes in v3:
time: 61.2 us; the launch traced here: 60.9 us
  blocking collectives  55.8 us (91%)
  Pallas kernels  2.6 us (4%)
  local copies, waits for them, and re-layouts  1.84 us (3%)
  between operations  0.67 us (1%)
    all_to_all x2, blocking collectives, exchange(): lax.all_to_all(array, 'rep', split_axis=0, concat_axis=0, tiled=True)  40.2 us
    all_to_all x1, blocking collectives, per_device(): lax.all_to_all(squares.reshape(shards, 1, LANES), ('rep', 'fsdp'), split_...  15.6 us
    unnamed x8, local copies, waits for them, and re-layouts  1.84 us

profile of v3, /device:TPU:1, one launch (start us, length us, event | category | flops | bytes accessed | tf_op | source)
XLA Modules:
  0.0 60.9 jit_solution(10014904048623337913)
XLA Ops:
  0.6 0.0 copy-start
  0.6 0.9 %copy-done = f32[4,14336]{1,0:T(4,128)S(1)} copy-done((f32[4,14336]{1,0:T(4,128)S(1)}, f32[4,14336]{1,0:T(4,128)}, u32[]{:S(2)}) %copy-start) | copy-done | bytes 229400
  1.6 0.0 copy-start.3
  1.6 0.9 %copy-done.3 = bf16[1,4,14336]{2,1,0:T(4,128)(2,1)S(1)} copy-done((bf16[1,4,14336]{2,1,0:T(4,128)(2,1)S(1)}, bf16[1,4,14336]{2,1,0:T(4,128)(2,1)}, u32[]{:S(2)}) %copy-start.3) | copy-done | bytes 114712
  2.5 0.7 %shard_map.50 = bf16[512,128]{1,0:T(8,128)(2,1)S(1)} custom-call(bf16[448,128]{1,0:T(8,128)(2,1)S(1)} %bitcast.40, f32[448,128]{1,0:T(8,128)S(1)} %bitcast.33), custom_call_target="tpu_custom_call" | custom-call | tf_op jit(solution)/shard_map/pallas_call | solution.py:147
  3.2 25.3 %all_to_all.15 = bf16[64,8,128]{2,1,0:T(8,128)(2,1)S(1)} all-to-all(bf16[64,8,128]{2,1,0:T(8,128)(2,1)S(1)} %bitcast.38), channel_id=1, replica_groups=mesh['rep'=64,'fsdp'=8] {'rep'}, dimensions={0} | all-to-all | bytes 262144 | tf_op jit(solution)/shard_map/all_to_all | solution.py:144
  28.5 0.0 copy-start.2
  28.5 0.7 %shard_map.51 = bf16[512,128]{1,0:T(8,128)(2,1)S(1)} custom-call(bf16[512,128]{1,0:T(8,128)(2,1)S(1)} %bitcast.36), custom_call_target="tpu_custom_call" | custom-call | tf_op jit(solution)/shard_map/pallas_call | solution.py:153
  29.3 0.0 copy-start.1
  29.3 14.8 %all_to_all.16 = bf16[64,8,128]{2,1,0:T(8,128)(2,1)S(1)} all-to-all(bf16[64,8,128]{2,1,0:T(8,128)(2,1)S(1)} %bitcast.37), channel_id=1, replica_groups=mesh['rep'=64,'fsdp'=8] {'rep'}, dimensions={0} | all-to-all | bytes 262144 | tf_op jit(solution)/shard_map/all_to_all | solution.py:144
  44.1 0.3 shard_map.52
  44.4 15.6 %all_to_all.17 = f32[8,1,128]{2,1,0:T(1,128)S(1)} all-to-all(f32[8,1,128]{2,1,0:T(1,128)S(1)} %bitcast.42), channel_id=1, replica_groups={{0,33,2,35,4,37,6,39},{8,41,10,43,12,45,14,47},{16,49,18,51,20,53,22,55..., dimensions={0} | all-to-all | bytes 8192 | tf_op jit(solution)/shard_map/all_to_all | solution.py:163
  60.1 0.0 copy-done.2
  60.1 0.0 copy-done.1
  60.1 0.8 %shard_map.53 = (f32[448,128]{1,0:T(8,128)}, f32[448,128]{1,0:T(8,128)}) custom-call(f32[448,128]{1,0:T(8,128)S(1)} %get-tuple-element.6.refs_0_, f32[448,128]{1,0:T(8,128)S(1)} %bitcast.34, f32[448,128]{1,0:T(8,128)S(1)} %bitcast.39, f32[8,128]{1,0:T(8,128)S(1)} %bitcast.41), custom_call_target="tpu_custom_call" | custom-call | tf_op jit(solution)/shard_map/pallas_call | solution.py:167
Async XLA Ops:
  0.6 0.9 %copy-start = (f32[4,14336]{1,0:T(4,128)S(1)}, f32[4,14336]{1,0:T(4,128)}, u32[]{:S(2)}) copy-start(f32[4,14336]{1,0:T(4,128)} %param.4) | copy-start | bytes 688132
  1.6 0.9 %copy-start.3 = (bf16[1,4,14336]{2,1,0:T(4,128)(2,1)S(1)}, bf16[1,4,14336]{2,1,0:T(4,128)(2,1)}, u32[]{:S(2)}) copy-start(bf16[1,4,14336]{2,1,0:T(4,128)(2,1)} %param.3) | copy-start | bytes 344068
  28.5 31.5 %copy-start.2 = (f32[4,14336]{1,0:T(4,128)S(1)}, f32[4,14336]{1,0:T(4,128)}, u32[]{:S(2)}) copy-start(f32[4,14336]{1,0:T(4,128)} %param.5) | copy-start | bytes 688132
  29.3 30.8 %copy-start.1 = (f32[4,14336]{1,0:T(4,128)S(1)}, f32[4,14336]{1,0:T(4,128)}, u32[]{:S(2)}) copy-start(f32[4,14336]{1,0:T(4,128)} %param.4) | copy-start | bytes 688132

commit v4 on v3

--- a/solution.py
+++ b/solution.py
@@ -180,7 +180,7 @@
 
     partner = {0: 6, 1: 7, 2: 4, 3: 5}
     return [
-        [index(y, z, core, x) for x in range(shards // 2) for z in (low, partner[low])]
+        [index(y, z, core ^ (z // 4), x) for x in range(shards // 2) for z in (low, partner[low])]
         for y in range(replicas // 8)
         for low in range(4)
         for core in range(2)

time: 61.2 us -> 62.1 us (1.015)
  blocking collectives: 55.8 us -> 56.7 us
    all_to_all x1, blocking collectives: 15.6 us -> 16.5 us  [per_device(): lax.all_to_all(squares.reshape(shards, 1, LANES), ('rep', 'fsdp'), split_...]
where the time goes in v4:
time: 62.1 us; the launch traced here: 61.8 us
  blocking collectives  56.7 us (91%)
  Pallas kernels  2.6 us (4%)
  local copies, waits for them, and re-layouts  1.84 us (3%)
  between operations  0.67 us (1%)
    all_to_all x2, blocking collectives, exchange(): lax.all_to_all(array, 'rep', split_axis=0, concat_axis=0, tiled=True)  40.2 us
    all_to_all x1, blocking collectives, per_device(): lax.all_to_all(squares.reshape(shards, 1, LANES), ('rep', 'fsdp'), split_...  16.5 us
    unnamed x8, local copies, waits for them, and re-layouts  1.84 us

profile of v4, /device:TPU:1, one launch (start us, length us, event | category | flops | bytes accessed | tf_op | source)
XLA Modules:
  0.0 61.8 jit_solution(3189425242110680715)
XLA Ops:
  0.6 0.0 copy-start
  0.6 0.9 %copy-done = f32[4,14336]{1,0:T(4,128)S(1)} copy-done((f32[4,14336]{1,0:T(4,128)S(1)}, f32[4,14336]{1,0:T(4,128)}, u32[]{:S(2)}) %copy-start) | copy-done | bytes 229400
  1.6 0.0 copy-start.3
  1.6 0.9 %copy-done.3 = bf16[1,4,14336]{2,1,0:T(4,128)(2,1)S(1)} copy-done((bf16[1,4,14336]{2,1,0:T(4,128)(2,1)S(1)}, bf16[1,4,14336]{2,1,0:T(4,128)(2,1)}, u32[]{:S(2)}) %copy-start.3) | copy-done | bytes 114712
  2.5 0.7 %shard_map.50 = bf16[512,128]{1,0:T(8,128)(2,1)S(1)} custom-call(bf16[448,128]{1,0:T(8,128)(2,1)S(1)} %bitcast.40, f32[448,128]{1,0:T(8,128)S(1)} %bitcast.33), custom_call_target="tpu_custom_call" | custom-call | tf_op jit(solution)/shard_map/pallas_call | solution.py:147
  3.2 25.3 %all_to_all.15 = bf16[64,8,128]{2,1,0:T(8,128)(2,1)S(1)} all-to-all(bf16[64,8,128]{2,1,0:T(8,128)(2,1)S(1)} %bitcast.38), channel_id=1, replica_groups=mesh['rep'=64,'fsdp'=8] {'rep'}, dimensions={0} | all-to-all | bytes 262144 | tf_op jit(solution)/shard_map/all_to_all | solution.py:144
  28.5 0.0 copy-start.2
  28.5 0.7 %shard_map.51 = bf16[512,128]{1,0:T(8,128)(2,1)S(1)} custom-call(bf16[512,128]{1,0:T(8,128)(2,1)S(1)} %bitcast.36), custom_call_target="tpu_custom_call" | custom-call | tf_op jit(solution)/shard_map/pallas_call | solution.py:153
  29.3 0.0 copy-start.1
  29.3 14.8 %all_to_all.16 = bf16[64,8,128]{2,1,0:T(8,128)(2,1)S(1)} all-to-all(bf16[64,8,128]{2,1,0:T(8,128)(2,1)S(1)} %bitcast.37), channel_id=1, replica_groups=mesh['rep'=64,'fsdp'=8] {'rep'}, dimensions={0} | all-to-all | bytes 262144 | tf_op jit(solution)/shard_map/all_to_all | solution.py:144
  44.1 0.3 shard_map.52
  44.4 16.5 %all_to_all.17 = f32[8,1,128]{2,1,0:T(1,128)S(1)} all-to-all(f32[8,1,128]{2,1,0:T(1,128)S(1)} %bitcast.42), channel_id=1, replica_groups={{0,41,2,43,4,45,6,47},{8,33,10,35,12,37,14,39},{16,57,18,59,20,61,22,63..., dimensions={0} | all-to-all | bytes 8192 | tf_op jit(solution)/shard_map/all_to_all | solution.py:163
  61.0 0.0 copy-done.2
  61.0 0.0 copy-done.1
  61.0 0.8 %shard_map.53 = (f32[448,128]{1,0:T(8,128)}, f32[448,128]{1,0:T(8,128)}) custom-call(f32[448,128]{1,0:T(8,128)S(1)} %get-tuple-element.6.refs_0_, f32[448,128]{1,0:T(8,128)S(1)} %bitcast.34, f32[448,128]{1,0:T(8,128)S(1)} %bitcast.39, f32[8,128]{1,0:T(8,128)S(1)} %bitcast.41), custom_call_target="tpu_custom_call" | custom-call | tf_op jit(solution)/shard_map/pallas_call | solution.py:167
Async XLA Ops:
  0.6 0.9 %copy-start = (f32[4,14336]{1,0:T(4,128)S(1)}, f32[4,14336]{1,0:T(4,128)}, u32[]{:S(2)}) copy-start(f32[4,14336]{1,0:T(4,128)} %param.4) | copy-start | bytes 688132
  1.6 0.9 %copy-start.3 = (bf16[1,4,14336]{2,1,0:T(4,128)(2,1)S(1)}, bf16[1,4,14336]{2,1,0:T(4,128)(2,1)}, u32[]{:S(2)}) copy-start(bf16[1,4,14336]{2,1,0:T(4,128)(2,1)} %param.3) | copy-start | bytes 344068
  28.5 32.4 %copy-start.2 = (f32[4,14336]{1,0:T(4,128)S(1)}, f32[4,14336]{1,0:T(4,128)}, u32[]{:S(2)}) copy-start(f32[4,14336]{1,0:T(4,128)} %param.5) | copy-start | bytes 688132
  29.3 31.7 %copy-start.1 = (f32[4,14336]{1,0:T(4,128)S(1)}, f32[4,14336]{1,0:T(4,128)}, u32[]{:S(2)}) copy-start(f32[4,14336]{1,0:T(4,128)} %param.4) | copy-start | bytes 688132

commit v5 on v2

v5 whole, which is shorter than its diff:
```python
import math

import jax
import jax.numpy as jnp
from jax import lax
from jax.experimental import pallas as pl
from jax.experimental.pallas import tpu as pltpu
from jax.sharding import PartitionSpec as P

QBLOCK = 32
LANES = 128
UNIT = 8
CHUNK = UNIT * UNIT
PARAMS = pltpu.CompilerParams(vmem_limit_bytes=4 << 20)

eps = 1e-06
clip_ratio = 0.2
outer_rate = 0.7
decay = 0.9

STAIR = (6.57973575592041, -12.987854957580566, 12.20757007598877, -6.687924861907959, 2.368926763534546, -0.5121700763702393)


def staircase(values):
    near = jnp.round(values)
    rest = values - near
    square = rest * rest
    poly = jnp.full_like(square, STAIR[-1])
    for coefficient in STAIR[-2::-1]:
        poly = poly * square + coefficient
    return near + rest * square * poly


def index_of(shape, axis):
    return lax.broadcasted_iota(jnp.int32, shape, axis)


def zero_one(condition):
    return jnp.where(condition, 1.0, 0.0).astype(jnp.bfloat16)


def block_ones():
    shape = (LANES, LANES)
    return zero_one(index_of(shape, 0) // QBLOCK == index_of(shape, 1) // QBLOCK)


def own_lane(shape):
    row, lane = index_of(shape, 0) % UNIT, index_of(shape, 1) % QBLOCK
    return (row == lane) & (row < UNIT - 1)


def dot(one, two):
    return jnp.dot(one.astype(jnp.bfloat16), two, preferred_element_type=jnp.float32)


def packed_top(arrays, lane):
    arrays = [jnp.abs(array) for array in arrays]
    shift = QBLOCK // 2
    while shift:
        halves = []
        for one, two in zip(arrays[::2], arrays[1::2]):
            one = jnp.maximum(one, pltpu.roll(one, shift, 1))
            two = jnp.maximum(two, pltpu.roll(two, LANES - shift, 1))
            halves.append(jnp.where(lane & shift != 0, one, two))
        arrays = halves
        shift //= 2
    return arrays[0]


def place_of(j):
    return sum((QBLOCK // 2) >> bit for bit in range(5) if not (j >> bit) & 1)


def swap(values, lane, shift):
    return jnp.where(lane & shift == 0, pltpu.roll(values, LANES - shift, 1), pltpu.roll(values, shift, 1))


def full_top(values, lane):
    top = jnp.abs(values)
    for shift in (1, 4):
        down = [pltpu.roll(top, LANES - shift * k, 1) for k in (1, 2, 3)]
        up = [pltpu.roll(top, shift * k, 1) for k in (1, 2, 3)]
        place = (lane // shift) % 4
        first = jnp.where(place < 3, down[0], up[0])
        second = jnp.where(place < 2, down[1], up[1])
        third = jnp.where(place == 0, down[2], jnp.where(place == 3, up[2], up[0]))
        top = jnp.maximum(jnp.maximum(top, first), jnp.maximum(second, third))
    return jnp.maximum(top, swap(top, lane, 16))


def scale_of(top):
    return ((top + eps) * (1.0 / 7.0)).astype(jnp.bfloat16).astype(jnp.float32)


def encode(values):
    shape = values.shape
    row, lane = index_of(shape, 0), index_of(shape, 1) % QBLOCK
    scale = scale_of(full_top(values, lane))
    code = staircase(values * pl.reciprocal(scale))
    line = jnp.sum(jnp.where(own_lane(shape), scale, 0.0), axis=0, keepdims=True)
    return jnp.where(row == UNIT - 1, line, code)


def decode(message, ones):
    shape = message.shape
    message = message.astype(jnp.float32)
    groups = (shape[0] // UNIT, UNIT, LANES)
    line = message.reshape(groups)[:, UNIT - 1 :, :]
    line = jnp.broadcast_to(line, groups).reshape(shape)
    return message * dot(jnp.where(own_lane(shape), line, 0.0), ones)


def first_kernel(local_ref, base_ref, out_ref, local_buffer, base_buffer, delta_ref, scale_ref, code_ref, sems):
    rows = base_ref.shape[0]
    step = rows // UNIT
    copies = [
        pltpu.make_async_copy(base_ref, base_buffer, sems.at[0]),
        pltpu.make_async_copy(local_ref, local_buffer, sems.at[1]),
    ]
    for copy in copies:
        copy.start()
    ones = block_ones()
    lane = index_of((UNIT, LANES), 1) % QBLOCK
    for copy in copies:
        copy.wait()
    delta_ref[:rows] = base_buffer[...] - local_buffer[...].astype(jnp.float32)
    pieces = [delta_ref[pl.ds(a * step + s, UNIT, stride=UNIT)] for a in range(UNIT) for s in range(UNIT)]
    scales = []
    for first in range(0, len(pieces), QBLOCK):
        scale = scale_of(packed_top(pieces[first : first + QBLOCK], lane))
        scales += [jnp.where(lane == place_of(j), scale, 0.0) for j in range(QBLOCK)]
    for a in range(UNIT):
        here = pl.ds(a * CHUNK, CHUNK)
        group = slice(a * UNIT, (a + 1) * UNIT)
        scale = dot(jnp.concatenate(scales[group], axis=0), ones)
        scale_ref[here] = scale
        code_ref[here] = staircase(jnp.concatenate(pieces[group], axis=0) * pl.reciprocal(scale))
        line = jnp.zeros((UNIT, LANES), jnp.float32)
        for s in range(UNIT - 1):
            line = jnp.where(lane == s, scale_ref[pl.ds(a * CHUNK + s, UNIT, stride=UNIT)], line)
        code_ref[pl.ds(a * CHUNK + UNIT - 1, UNIT, stride=UNIT)] = line
        out_ref[here] = code_ref[here].astype(jnp.bfloat16)


def second_kernel(in_ref, out_ref, *, replicas):
    ones = block_ones()
    total = jnp.zeros((UNIT, LANES), jnp.float32)
    values = decode(in_ref[...], ones)
    total += jnp.sum(values.reshape(CHUNK, UNIT, LANES), axis=0)
    message = jnp.concatenate([encode(total / replicas)] * UNIT, axis=0).astype(jnp.bfloat16)
    for a in range(UNIT):
        out_ref[a * CHUNK : (a + 1) * CHUNK] = message


def third_kernel(in_ref, grad_ref, squares_ref):
    ones = block_ones()
    step = grad_ref.shape[0] // UNIT
    total = jnp.zeros((UNIT, LANES), jnp.float32)
    values = decode(in_ref[...], ones)
    total += jnp.sum((values * values).reshape(CHUNK, UNIT, LANES), axis=0)
    for a in range(UNIT):
        for s in range(UNIT):
            first = (a * UNIT + s) * UNIT
            grad_ref[pl.ds(a * step + s, UNIT - 1, stride=UNIT)] = values[first : first + UNIT - 1]
    squares_ref[...] = jnp.full((UNIT, LANES), jnp.sum(total), jnp.float32)


def fourth_kernel(grad_ref, base_ref, momentum_ref, squares_ref, new_base_ref, new_momentum_ref, *, limit):
    squares = jnp.sum(squares_ref[...], axis=0, keepdims=True)
    factor = limit / jnp.maximum(jnp.sqrt(squares), limit)
    scaled = factor * grad_ref[...]
    momentum = decay * momentum_ref[...] + scaled
    new_momentum_ref[...] = momentum
    new_base_ref[...] = base_ref[...] - outer_rate * (scaled + decay * momentum)


def to_units(array):
    rows, width = array.shape
    return array.reshape(rows, width // LANES, LANES).transpose(1, 0, 2).reshape(rows * width // LANES, LANES)


def from_units(array, rows, width):
    return array.reshape(width // LANES, rows, LANES).transpose(1, 0, 2).reshape(rows, width)


def run_first(local_units, base_units):
    units = base_units.shape[0]
    return pl.pallas_call(
        first_kernel, name="encode_pieces",
        compiler_params=PARAMS,
        in_specs=[pl.BlockSpec(memory_space=pltpu.HBM)] * 2,
        out_shape=jax.ShapeDtypeStruct((CHUNK * UNIT, LANES), jnp.bfloat16),
        scratch_shapes=[
            pltpu.VMEM((units, LANES), jnp.bfloat16),
            pltpu.VMEM((units, LANES), jnp.float32),
            pltpu.VMEM((units + CHUNK, LANES), jnp.float32),
            pltpu.VMEM((CHUNK * UNIT, LANES), jnp.float32),
            pltpu.VMEM((CHUNK * UNIT, LANES), jnp.float32),
            pltpu.SemaphoreType.DMA((2,)),
        ],
    )(*(pltpu.with_memory_space_constraint(array, pltpu.HBM) for array in (local_units, base_units)))


def run_second(message, replicas):
    return pl.pallas_call(
        lambda *refs: second_kernel(*refs, replicas=replicas),name="add_and_encode",
        compiler_params=PARAMS,
        out_shape=jax.ShapeDtypeStruct((CHUNK * UNIT, LANES), jnp.bfloat16),
    )(message)


def run_third(message, units):
    return pl.pallas_call(
        third_kernel, name="decode_all",
        compiler_params=PARAMS,
        out_shape=(jax.ShapeDtypeStruct((units, LANES), jnp.float32), jax.ShapeDtypeStruct((UNIT, LANES), jnp.float32)),
    )(message)


def run_fourth(grad, base_units, momentum_units, squares, limit):
    units = base_units.shape[0]
    return pl.pallas_call(
        lambda *refs: fourth_kernel(*refs, limit=limit),
        compiler_params=PARAMS,
        name="update",
        out_shape=(jax.ShapeDtypeStruct((units, LANES), jnp.float32),) * 2,
    )(grad, base_units, momentum_units, squares)


def per_device(groups, local_params, base, momentum):
    replicas = lax.axis_size("rep")
    shards = lax.axis_size("fsdp")
    rows, width = base.shape

    def exchange(array):
        array = array.reshape(replicas, UNIT, LANES)
        return lax.all_to_all(array, "rep", split_axis=0, concat_axis=0, tiled=True).reshape(replicas * UNIT, LANES)

    base_units = to_units(base)
    pieces = run_first(to_units(local_params[0]), base_units)
    owned = run_second(exchange(pieces), replicas)
    grad, squares = run_third(exchange(owned), base_units.shape[0])
    squares = lax.all_to_all(
        squares.reshape(shards, 1, LANES), ("rep", "fsdp"), split_axis=0, concat_axis=0, tiled=True, axis_index_groups=groups
    ).reshape(shards, LANES)
    limit = clip_ratio * float(rows * width * shards) ** 0.5
    new_base, new_momentum = run_fourth(grad, base_units, to_units(momentum), squares, limit)
    return from_units(new_base, rows, width), from_units(new_momentum, rows, width)


def near_groups(mesh):
    replicas, shards = mesh.shape["rep"], mesh.shape["fsdp"]

    def index(y, z, core, x):
        return ((y * 4 + z % 4) * 2 + core) * shards + x * 2 + z // 4

    partner = {0: 6, 1: 7, 2: 4, 3: 5}
    return [
        [index(y, z, core, x) for x in range(shards // 2) for z in (low, partner[low])]
        for y in range(replicas // 8)
        for low in range(4)
        for core in range(2)
    ]


def solution(mesh):
    groups = near_groups(mesh)
    return jax.shard_map(
        lambda *arrays: per_device(groups, *arrays),
        mesh=mesh,
        in_specs=(P("rep", "fsdp", None), P("fsdp", None), P("fsdp", None)),
        out_specs=(P("fsdp", None), P("fsdp", None)),
        check_vma=False,
    )
```

time: 67.1 us -> 60.1 us (0.90)
  Pallas kernels: 8.5 us -> 3.39 us
  blocking collectives: 57.7 us -> 55.8 us
    pallas_call x4, Pallas kernels: 8.5 us -> 3.39 us  [the longest x1 1.77 us: run_first(): pl.pallas_call(first_kernel, name='encode_pieces', compiler_params=PARAMS...]
    all_to_all x2, blocking collectives: 41.9 us -> 40.2 us  [exchange(): lax.all_to_all(array, 'rep', split_axis=0, concat_axis=0, tiled=True)]
where the time goes in v5:
time: 60.1 us; the launch traced here: 59.9 us
  blocking collectives  55.8 us (93%)
  Pallas kernels  3.39 us (6%)
  between operations  0.66 us (1%)
    all_to_all x2, blocking collectives, exchange(): lax.all_to_all(array, 'rep', split_axis=0, concat_axis=0, tiled=True)  40.2 us
    all_to_all x1, blocking collectives, per_device(): lax.all_to_all(squares.reshape(shards, 1, LANES), ('rep', 'fsdp'), split_...  15.6 us
    pallas_call x1, Pallas kernels, run_first(): pl.pallas_call(first_kernel, name='encode_pieces', compiler_params=PARAMS...  1.77 us

profile of v5, /device:TPU:1, one launch (start us, length us, event | category | flops | bytes accessed | tf_op | source)
XLA Modules:
  0.0 59.9 jit_solution(11180433276399623690)
XLA Ops:
  0.6 1.8 %encode_pieces.1 = bf16[512,128]{1,0:T(8,128)(2,1)S(1)} custom-call(bf16[448,128]{1,0:T(8,128)(2,1)} %bitcast.42, f32[448,128]{1,0:T(8,128)} %bitcast.33), custom_call_target="tpu_custom_call" | custom-call | tf_op jit(solution)/shard_map/encode_pieces/pallas_call | solution.py:188
  2.4 25.3 %all_to_all.15 = bf16[64,8,128]{2,1,0:T(8,128)(2,1)S(1)} all-to-all(bf16[64,8,128]{2,1,0:T(8,128)(2,1)S(1)} %bitcast.38), channel_id=1, replica_groups=mesh['rep'=64,'fsdp'=8] {'rep'}, dimensions={0} | all-to-all | bytes 262144 | tf_op jit(solution)/shard_map/all_to_all | solution.py:237
  27.7 0.0 copy-start.1
  27.7 0.5 add_and_encode.1
  28.2 0.0 copy-start
  28.2 14.8 %all_to_all.16 = bf16[64,8,128]{2,1,0:T(8,128)(2,1)S(1)} all-to-all(bf16[64,8,128]{2,1,0:T(8,128)(2,1)S(1)} %bitcast.37), channel_id=1, replica_groups=mesh['rep'=64,'fsdp'=8] {'rep'}, dimensions={0} | all-to-all | bytes 262144 | tf_op jit(solution)/shard_map/all_to_all | solution.py:237
  43.1 0.3 decode_all.1
  43.4 15.6 %all_to_all.17 = f32[8,1,128]{2,1,0:T(1,128)S(1)} all-to-all(f32[8,1,128]{2,1,0:T(1,128)S(1)} %bitcast.41), channel_id=1, replica_groups={{0,33,2,35,4,37,6,39},{8,41,10,43,12,45,14,47},{16,49,18,51,20,53,22,55..., dimensions={0} | all-to-all | bytes 8192 | tf_op jit(solution)/shard_map/all_to_all | solution.py:243
  59.0 0.0 copy-done.1
  59.0 0.0 copy-done
  59.0 0.8 %update.1 = (f32[448,128]{1,0:T(8,128)}, f32[448,128]{1,0:T(8,128)}) custom-call(f32[448,128]{1,0:T(8,128)S(1)} %get-tuple-element.6.refs_0_, f32[448,128]{1,0:T(8,128)S(1)} %bitcast.34, f32[448,128]{1,0:T(8,128)S(1)} %bitcast.39, f32[8,128]{1,0:T(8,128)S(1)} %bitcast.40), custom_call_target="tpu_custom_call" | custom-call | tf_op jit(solution)/shard_map/update/pallas_call | solution.py:222
Async XLA Ops:
  27.7 31.3 %copy-start.1 = (f32[4,14336]{1,0:T(4,128)S(1)}, f32[4,14336]{1,0:T(4,128)}, u32[]{:S(2)}) copy-start(f32[4,14336]{1,0:T(4,128)} %param.5) | copy-start | bytes 688132
  28.2 30.8 %copy-start = (f32[4,14336]{1,0:T(4,128)S(1)}, f32[4,14336]{1,0:T(4,128)}, u32[]{:S(2)}) copy-start(f32[4,14336]{1,0:T(4,128)} %param.4) | copy-start | bytes 688132

commit v6 on v2

v6 whole, which is shorter than its diff:
```python
import math

import jax
import jax.numpy as jnp
from jax import lax
from jax.experimental import pallas as pl
from jax.experimental.pallas import tpu as pltpu
from jax.sharding import PartitionSpec as P

QBLOCK = 32
LANES = 128
UNIT = 8
PARAMS = pltpu.CompilerParams(vmem_limit_bytes=4 << 20)

eps = 1e-06
clip_ratio = 0.2
outer_rate = 0.7
decay = 0.9

SUM_TYPE = jnp.float16
SUM_SCALE = 4.0

STAIR = (6.57973575592041, -12.987854957580566, 12.20757007598877, -6.687924861907959, 2.368926763534546, -0.5121700763702393)


def staircase(values):
    near = jnp.round(values)
    rest = values - near
    square = rest * rest
    poly = jnp.full_like(square, STAIR[-1])
    for coefficient in STAIR[-2::-1]:
        poly = poly * square + coefficient
    return near + rest * square * poly


def rounded(values):
    return values.astype(jnp.bfloat16).astype(jnp.float32)


def scale_of(top):
    return rounded((top + eps) * (1.0 / 7.0))


def code_of(values, scale):
    return rounded(staircase(values * pl.reciprocal(scale)))


def index_of(shape, axis):
    return lax.broadcasted_iota(jnp.int32, shape, axis)


def block_ones():
    shape = (LANES, LANES)
    return jnp.where(index_of(shape, 0) // QBLOCK == index_of(shape, 1) // QBLOCK, 1.0, 0.0).astype(jnp.bfloat16)


def spread(values, ones):
    return jnp.dot(values.astype(jnp.bfloat16), ones, preferred_element_type=jnp.float32)


def packed_top(arrays, lane):
    arrays = [jnp.abs(array) for array in arrays]
    shift = QBLOCK // 2
    while shift:
        if len(arrays) % 2:
            arrays.append(jnp.zeros_like(arrays[0]))
        halves = []
        for one, two in zip(arrays[::2], arrays[1::2]):
            one = jnp.maximum(one, pltpu.roll(one, shift, 1))
            two = jnp.maximum(two, pltpu.roll(two, LANES - shift, 1))
            halves.append(jnp.where(lane & shift != 0, one, two))
        arrays = halves
        shift //= 2
    return arrays[0]


def place_of(j):
    return sum((QBLOCK // 2) >> bit for bit in range(5) if not (j >> bit) & 1)


def full_top(values, lane):
    top = jnp.abs(values)
    for shift in (1, 4):
        down = [pltpu.roll(top, LANES - shift * k, 1) for k in (1, 2, 3)]
        up = [pltpu.roll(top, shift * k, 1) for k in (1, 2, 3)]
        place = (lane // shift) % 4
        first = jnp.where(place < 3, down[0], up[0])
        second = jnp.where(place < 2, down[1], up[1])
        third = jnp.where(place == 0, down[2], jnp.where(place == 3, up[2], up[0]))
        top = jnp.maximum(jnp.maximum(top, first), jnp.maximum(second, third))
    return jnp.maximum(top, jnp.where(lane < 16, pltpu.roll(top, LANES - 16, 1), pltpu.roll(top, 16, 1)))


def first_kernel(local_ref, base_ref, out_ref):
    rows = base_ref.shape[0] // UNIT
    ones = block_ones()
    lane = index_of((UNIT, LANES), 1) % QBLOCK
    mine = lax.rem(lax.axis_index("rep"), UNIT)
    base = base_ref[pl.ds(pl.multiple_of(mine * rows, UNIT), rows)]
    local = local_ref[...].astype(jnp.float32)
    starts = range(0, rows, UNIT)
    deltas = [base[i : i + UNIT] - local[j * rows + i : j * rows + i + UNIT] for j in range(UNIT) for i in starts]
    scales = []
    for first in range(0, len(deltas), QBLOCK):
        group = deltas[first : first + QBLOCK]
        scale = scale_of(packed_top(group, lane))
        scales += [jnp.where(lane == place_of(j), scale, 0.0) for j in range(len(group))]
    total = jnp.zeros((rows, LANES), jnp.float32)
    count = len(starts)
    for j in range(UNIT):
        here = slice(j * count, (j + 1) * count)
        scale = spread(jnp.concatenate(scales[here], axis=0), ones)
        total += code_of(jnp.concatenate(deltas[here], axis=0), scale) * scale
    total *= SUM_SCALE
    for j in range(UNIT):
        out_ref[j * rows : (j + 1) * rows] = total


def second_kernel(in_ref, out_ref, *, replicas):
    rows = in_ref.shape[0] // UNIT
    total = in_ref[:rows]
    for j in range(1, UNIT):
        total += in_ref[j * rows : (j + 1) * rows]
    average = total * (1.0 / (replicas * SUM_SCALE))
    lane = index_of(average.shape, 1) % QBLOCK
    row = index_of(average.shape, 0) % UNIT
    scale = scale_of(full_top(average, lane))
    code = code_of(average, scale)
    own = jnp.where(lane == row, scale, 0.0)
    place = index_of((UNIT, LANES), 0)
    lines = jnp.zeros((UNIT, LANES), jnp.float32)
    for i in range(rows // UNIT):
        line = jnp.sum(own[i * UNIT : (i + 1) * UNIT], axis=0, keepdims=True)
        lines = jnp.where(place == i, line, lines)
    message = jnp.concatenate([code, lines], axis=0).astype(jnp.bfloat16)
    size = rows + UNIT
    for j in range(UNIT):
        out_ref[j * size : (j + 1) * size] = message


def third_kernel(in_ref, grad_ref, squares_ref):
    ones = block_ones()
    size, rows = in_ref.shape[0] // UNIT, grad_ref.shape[0] // UNIT
    shape = (UNIT, LANES)
    own = index_of(shape, 0) == index_of(shape, 1) % QBLOCK
    total = jnp.zeros(shape, jnp.float32)
    for j in range(UNIT):
        message = in_ref[j * size : (j + 1) * size].astype(jnp.float32)
        scales = [
            jnp.where(own, jnp.broadcast_to(message[rows + i : rows + i + 1], shape), 0.0) for i in range(rows // UNIT)
        ]
        values = message[:rows] * spread(jnp.concatenate(scales, axis=0), ones)
        grad_ref[j * rows : (j + 1) * rows] = values
        total += jnp.sum((values * values).reshape(rows // UNIT, UNIT, LANES), axis=0)
    squares_ref[...] = jnp.full(shape, jnp.sum(total), jnp.float32)


def fourth_kernel(grad_ref, base_ref, momentum_ref, squares_ref, new_base_ref, new_momentum_ref, *, limit):
    squares = jnp.sum(squares_ref[...], axis=0, keepdims=True)
    factor = limit / jnp.maximum(jnp.sqrt(squares), limit)
    scaled = factor * grad_ref[...]
    momentum = decay * momentum_ref[...] + scaled
    new_momentum_ref[...] = momentum
    new_base_ref[...] = base_ref[...] - outer_rate * (scaled + decay * momentum)


def to_units(array):
    rows, width = array.shape
    return array.reshape(rows, width // LANES, LANES).transpose(1, 0, 2).reshape(rows * width // LANES, LANES)


def from_units(array, rows, width):
    return array.reshape(width // LANES, rows, LANES).transpose(1, 0, 2).reshape(rows, width)


def call(kernel, name, out_shape, *operands):
    return pl.pallas_call(kernel, name=name, compiler_params=PARAMS, out_shape=out_shape)(*operands)


def per_device(groups, local_params, base, momentum):
    replicas = lax.axis_size("rep")
    shards = lax.axis_size("fsdp")
    rows, width = base.shape
    units = rows * width // LANES
    planes = [[y * UNIT + q for q in range(UNIT)] for y in range(replicas // UNIT)]
    lines = [[y * UNIT + q for y in range(replicas // UNIT)] for q in range(UNIT)]

    def exchange(array, peers):
        return lax.all_to_all(array, "rep", split_axis=0, concat_axis=0, tiled=True, axis_index_groups=peers)

    def shape(count, dtype=jnp.float32):
        return jax.ShapeDtypeStruct((count, LANES), dtype)

    base_units = to_units(base)
    local = local_params[0].reshape(rows, width // LANES, LANES).transpose(1, 0, 2)
    local = exchange(local, planes).reshape(units, LANES)
    sums = call(first_kernel, "quantize_and_add", shape(units), local, base_units)
    sums = exchange(sums.astype(SUM_TYPE).reshape(UNIT, units // UNIT, LANES), lines)
    sums = sums.reshape(units, LANES).astype(jnp.float32)
    size = units // UNIT + UNIT
    message = call(lambda *refs: second_kernel(*refs, replicas=replicas), "average_and_encode", shape(UNIT * size, jnp.bfloat16), sums)
    message = exchange(message.reshape(UNIT, size, LANES), planes).reshape(UNIT * size, LANES)
    grad, squares = call(third_kernel, "decode_all", (shape(units), shape(shards)), message)
    squares = lax.all_to_all(
        squares.reshape(shards, 1, LANES), ("rep", "fsdp"), split_axis=0, concat_axis=0, tiled=True, axis_index_groups=groups
    ).reshape(shards, LANES)
    limit = clip_ratio * float(rows * width * shards) ** 0.5
    new_base, new_momentum = call(
        lambda *refs: fourth_kernel(*refs, limit=limit),
        "update",
        (shape(units), shape(units)),
        grad,
        base_units,
        to_units(momentum),
        squares,
    )
    return from_units(new_base, rows, width), from_units(new_momentum, rows, width)


def near_groups(mesh):
    replicas, shards = mesh.shape["rep"], mesh.shape["fsdp"]

    def index(y, z, core, x):
        return ((y * 4 + z % 4) * 2 + core) * shards + x * 2 + z // 4

    partner = {0: 6, 1: 7, 2: 4, 3: 5}
    return [
        [index(y, z, core, x) for x in range(shards // 2) for z in (low, partner[low])]
        for y in range(replicas // 8)
        for low in range(4)
        for core in range(2)
    ]


def solution(mesh):
    groups = near_groups(mesh)
    return jax.shard_map(
        lambda *arrays: per_device(groups, *arrays),
        mesh=mesh,
        in_specs=(P("rep", "fsdp", None), P("fsdp", None), P("fsdp", None)),
        out_specs=(P("fsdp", None), P("fsdp", None)),
        check_vma=False,
    )
```

time: 67.1 us -> 57.6 us (0.86)
  Pallas kernels: 8.5 us -> 2.2 us
  blocking collectives: 57.7 us -> 54.1 us
    pallas_call x4, Pallas kernels: 8.5 us -> 2.2 us  [call(): pl.pallas_call(kernel, name=name, compiler_params=PARAMS, out_shape=out_s...]
    all_to_all x2 -> x3, blocking collectives: 41.9 us -> 39.6 us  [exchange(): lax.all_to_all(array, 'rep', split_axis=0, concat_axis=0, tiled=True, axi...]
    all_to_all x1, blocking collectives: 15.8 us -> 14.5 us  [per_device(): lax.all_to_all(squares.reshape(shards, 1, LANES), ('rep', 'fsdp'), split_...]
where the time goes in v6:
time: 57.6 us; the launch traced here: 57.1 us
  blocking collectives  54.1 us (94%)
  Pallas kernels  2.2 us (4%)
  between operations  0.68 us (1%)
    all_to_all x3, blocking collectives, exchange(): lax.all_to_all(array, 'rep', split_axis=0, concat_axis=0, tiled=True, axi...  39.6 us
    all_to_all x1, blocking collectives, per_device(): lax.all_to_all(squares.reshape(shards, 1, LANES), ('rep', 'fsdp'), split_...  14.5 us
    pallas_call x4, Pallas kernels, call(): pl.pallas_call(kernel, name=name, compiler_params=PARAMS, out_shape=out_s...  2.2 us

profile of v6, /device:TPU:1, one launch (start us, length us, event | category | flops | bytes accessed | tf_op | source)
XLA Modules:
  0.0 57.1 jit_solution(9808355531966843862)
XLA Ops:
  0.6 0.0 copy-start
  0.6 16.0 %all_to_all.20 = bf16[112,4,128]{2,1,0:T(4,128)(2,1)S(1)} all-to-all(bf16[112,4,128]{2,1,0:T(4,128)(2,1)} %bitcast.43), channel_id=1, replica_groups={{0,8,16,24,32,40,48,56},{64,72,80,88,96,104,112,120},{128,136,144,152,1..., dimensions={0} | all-to-all | bytes 229376 | tf_op jit(solution)/shard_map/all_to_all | solution.py:189
  16.6 0.0 copy-done
  16.6 0.7 %quantize_and_add.1 = f32[448,128]{1,0:T(8,128)S(1)} custom-call(bf16[448,128]{1,0:T(8,128)(2,1)S(1)} %bitcast.38, f32[448,128]{1,0:T(8,128)S(1)} %bitcast.34), custom_call_target="tpu_custom_call" | custom-call | tf_op jit(solution)/shard_map/quantize_and_add/pallas_call | solution.py:177
  17.4 13.1 %all_to_all.21 = f16[8,56,128]{2,1,0:T(8,128)(2,1)S(1)} all-to-all(f16[8,56,128]{2,1,0:T(8,128)(2,1)S(1)} %bitcast.42), channel_id=1, replica_groups={{0,64,128,192,256,320,384,448},{8,72,136,200,264,328,392,456},{16,80,14..., dimensions={0} | all-to-all | bytes 229376 | tf_op jit(solution)/shard_map/all_to_all | solution.py:189
  30.5 0.3 average_and_encode.1
  30.8 0.0 copy-start.1
  30.8 10.5 %all_to_all.22 = bf16[8,64,128]{2,1,0:T(8,128)(2,1)S(1)} all-to-all(bf16[8,64,128]{2,1,0:T(8,128)(2,1)S(1)} %bitcast.37), channel_id=1, replica_groups={{0,8,16,24,32,40,48,56},{64,72,80,88,96,104,112,120},{128,136,144,152,1..., dimensions={0} | all-to-all | bytes 262144 | tf_op jit(solution)/shard_map/all_to_all | solution.py:189
  41.4 0.3 decode_all.1
  41.7 14.5 %all_to_all.23 = f32[8,1,128]{2,1,0:T(1,128)S(1)} all-to-all(f32[8,1,128]{2,1,0:T(1,128)S(1)} %bitcast.41), channel_id=1, replica_groups={{0,33,2,35,4,37,6,39},{8,41,10,43,12,45,14,47},{16,49,18,51,20,53,22,55..., dimensions={0} | all-to-all | bytes 8192 | tf_op jit(solution)/shard_map/all_to_all | solution.py:204
  56.2 0.0 copy-done.1
  56.2 0.8 %update.1 = (f32[448,128]{1,0:T(8,128)}, f32[448,128]{1,0:T(8,128)}) custom-call(f32[448,128]{1,0:T(8,128)S(1)} %get-tuple-element.6.refs_0_, f32[448,128]{1,0:T(8,128)S(1)} %bitcast.35, f32[448,128]{1,0:T(8,128)S(1)} %bitcast.39, f32[8,128]{1,0:T(8,128)S(1)} %bitcast.40), custom_call_target="tpu_custom_call" | custom-call | tf_op jit(solution)/shard_map/update/pallas_call | solution.py:177
  (2 shorter events, 0.0 us)
Async XLA Ops:
  0.6 16.0 %copy-start = (f32[4,14336]{1,0:T(4,128)S(1)}, f32[4,14336]{1,0:T(4,128)}, u32[]{:S(2)}) copy-start(f32[4,14336]{1,0:T(4,128)} %param.4) | copy-start | bytes 688132
  30.8 25.4 %copy-start.1 = (f32[4,14336]{1,0:T(4,128)S(1)}, f32[4,14336]{1,0:T(4,128)}, u32[]{:S(2)}) copy-start(f32[4,14336]{1,0:T(4,128)} %param.5) | copy-start | bytes 688132

commit v7 on v6

--- a/solution.py
+++ b/solution.py
@@ -17,8 +17,9 @@
 outer_rate = 0.7
 decay = 0.9
 
-SUM_TYPE = jnp.float16
-SUM_SCALE = 4.0
+SENT = jnp.float16
+SUM_FACTOR = 512.0
+GRAD_FACTOR = 1024.0
 
 STAIR = (6.57973575592041, -12.987854957580566, 12.20757007598877, -6.687924861907959, 2.368926763534546, -0.5121700763702393)
 
@@ -43,6 +44,16 @@
 
 def code_of(values, scale):
     return rounded(staircase(values * pl.reciprocal(scale)))
+
+
+def to_root(values, factor):
+    root = jnp.sqrt(jnp.abs(values)) * factor
+    return jnp.where(values < 0.0, -root, root)
+
+
+def from_root(root, factor):
+    root = root * (1.0 / factor)
+    return root * jnp.abs(root)
 
 
 def index_of(shape, axis):
@@ -111,48 +122,28 @@
         here = slice(j * count, (j + 1) * count)
         scale = spread(jnp.concatenate(scales[here], axis=0), ones)
         total += code_of(jnp.concatenate(deltas[here], axis=0), scale) * scale
-    total *= SUM_SCALE
+    total = to_root(total, SUM_FACTOR)
     for j in range(UNIT):
         out_ref[j * rows : (j + 1) * rows] = total
 
 
 def second_kernel(in_ref, out_ref, *, replicas):
     rows = in_ref.shape[0] // UNIT
-    total = in_ref[:rows]
+    total = from_root(in_ref[:rows], SUM_FACTOR)
     for j in range(1, UNIT):
-        total += in_ref[j * rows : (j + 1) * rows]
-    average = total * (1.0 / (replicas * SUM_SCALE))
-    lane = index_of(average.shape, 1) % QBLOCK
-    row = index_of(average.shape, 0) % UNIT
-    scale = scale_of(full_top(average, lane))
-    code = code_of(average, scale)
-    own = jnp.where(lane == row, scale, 0.0)
-    place = index_of((UNIT, LANES), 0)
-    lines = jnp.zeros((UNIT, LANES), jnp.float32)
-    for i in range(rows // UNIT):
-        line = jnp.sum(own[i * UNIT : (i + 1) * UNIT], axis=0, keepdims=True)
-        lines = jnp.where(place == i, line, lines)
-    message = jnp.concatenate([code, lines], axis=0).astype(jnp.bfloat16)
-    size = rows + UNIT
+        total += from_root(in_ref[j * rows : (j + 1) * rows], SUM_FACTOR)
+    average = total * (1.0 / replicas)
+    scale = scale_of(full_top(average, index_of(average.shape, 1) % QBLOCK))
+    message = to_root(code_of(average, scale) * scale, GRAD_FACTOR)
     for j in range(UNIT):
-        out_ref[j * size : (j + 1) * size] = message
+        out_ref[j * rows : (j + 1) * rows] = message
 
 
 def third_kernel(in_ref, grad_ref, squares_ref):
-    ones = block_ones()
-    size, rows = in_ref.shape[0] // UNIT, grad_ref.shape[0] // UNIT
-    shape = (UNIT, LANES)
-    own = index_of(shape, 0) == index_of(shape, 1) % QBLOCK
-    total = jnp.zeros(shape, jnp.float32)
-    for j in range(UNIT):
-        message = in_ref[j * size : (j + 1) * size].astype(jnp.float32)
-        scales = [
-            jnp.where(own, jnp.broadcast_to(message[rows + i : rows + i + 1], shape), 0.0) for i in range(rows // UNIT)
-        ]
-        values = message[:rows] * spread(jnp.concatenate(scales, axis=0), ones)
-        grad_ref[j * rows : (j + 1) * rows] = values
-        total += jnp.sum((values * values).reshape(rows // UNIT, UNIT, LANES), axis=0)
-    squares_ref[...] = jnp.full(shape, jnp.sum(total), jnp.float32)
+    grad = from_root(in_ref[...], GRAD_FACTOR)
+    grad_ref[...] = grad
+    total = jnp.sum((grad * grad).reshape(-1, UNIT, LANES), axis=0)
+    squares_ref[...] = jnp.full((UNIT, LANES), jnp.sum(total), jnp.float32)
 
 
 def fourth_kernel(grad_ref, base_ref, momentum_ref, squares_ref, new_base_ref, new_momentum_ref, *, limit):
@@ -188,19 +179,21 @@
     def exchange(array, peers):
         return lax.all_to_all(array, "rep", split_axis=0, concat_axis=0, tiled=True, axis_index_groups=peers)
 
-    def shape(count, dtype=jnp.float32):
-        return jax.ShapeDtypeStruct((count, LANES), dtype)
+    def exchange_roots(array, peers):
+        array = exchange(array.astype(SENT).reshape(UNIT, units // UNIT, LANES), peers)
+        return array.reshape(units, LANES).astype(jnp.float32)
+
+    def shape(count):
+        return jax.ShapeDtypeStruct((count, LANES), jnp.float32)
 
     base_units = to_units(base)
     local = local_params[0].reshape(rows, width // LANES, LANES).transpose(1, 0, 2)
     local = exchange(local, planes).reshape(units, LANES)
     sums = call(first_kernel, "quantize_and_add", shape(units), local, base_units)
-    sums = exchange(sums.astype(SUM_TYPE).reshape(UNIT, units // UNIT, LANES), lines)
-    sums = sums.reshape(units, LANES).astype(jnp.float32)
-    size = units // UNIT + UNIT
-    message = call(lambda *refs: second_kernel(*refs, replicas=replicas), "average_and_encode", shape(UNIT * size, jnp.bfloat16), sums)
-    message = exchange(message.reshape(UNIT, size, LANES), planes).reshape(UNIT * size, LANES)
-    grad, squares = call(third_kernel, "decode_all", (shape(units), shape(shards)), message)
+    sums = exchange_roots(sums, lines)
+    parts = call(lambda *refs: second_kernel(*refs, replicas=replicas), "average_and_quantize", shape(units), sums)
+    parts = exchange_roots(parts, planes)
+    grad, squares = call(third_kernel, "grad_and_squares", (shape(units), shape(shards)), parts)
     squares = lax.all_to_all(
         squares.reshape(shards, 1, LANES), ("rep", "fsdp"), split_axis=0, concat_axis=0, tiled=True, axis_index_groups=groups
     ).reshape(shards, LANES)

time: 57.6 us -> 57.2 us (level)
  no operation moved by 1% of the time
where the time goes in v7:
time: 57.2 us; the launch traced here: 56.9 us
  blocking collectives  54 us (94%)
  Pallas kernels  2.13 us (4%)
  between operations  0.69 us (1%)
    all_to_all x3, blocking collectives, exchange(): lax.all_to_all(array, 'rep', split_axis=0, concat_axis=0, tiled=True, axi...  39.3 us
    all_to_all x1, blocking collectives, per_device(): lax.all_to_all(squares.reshape(shards, 1, LANES), ('rep', 'fsdp'), split_...  14.6 us
    pallas_call x4, Pallas kernels, call(): pl.pallas_call(kernel, name=name, compiler_params=PARAMS, out_shape=out_s...  2.13 us

profile of v7, /device:TPU:1, one launch (start us, length us, event | category | flops | bytes accessed | tf_op | source)
XLA Modules:
  0.0 56.9 jit_solution(14613966681814420817)
XLA Ops:
  0.6 0.0 copy-start
  0.6 16.0 %all_to_all.20 = bf16[112,4,128]{2,1,0:T(4,128)(2,1)S(1)} all-to-all(bf16[112,4,128]{2,1,0:T(4,128)(2,1)} %bitcast.44), channel_id=1, replica_groups={{0,8,16,24,32,40,48,56},{64,72,80,88,96,104,112,120},{128,136,144,152,1..., dimensions={0} | all-to-all | bytes 229376 | tf_op jit(solution)/shard_map/all_to_all | solution.py:180
  16.6 0.0 copy-done
  16.6 0.7 %quantize_and_add.1 = f32[448,128]{1,0:T(8,128)S(1)} custom-call(bf16[448,128]{1,0:T(8,128)(2,1)S(1)} %bitcast.38, f32[448,128]{1,0:T(8,128)S(1)} %bitcast.36), custom_call_target="tpu_custom_call" | custom-call | tf_op jit(solution)/shard_map/quantize_and_add/pallas_call | solution.py:168
  17.4 13.1 %all_to_all.21 = f16[8,56,128]{2,1,0:T(8,128)(2,1)S(1)} all-to-all(f16[8,56,128]{2,1,0:T(8,128)(2,1)S(1)} %bitcast.42), channel_id=1, replica_groups={{0,64,128,192,256,320,384,448},{8,72,136,200,264,328,392,456},{16,80,14..., dimensions={0} | all-to-all | bytes 229376 | tf_op jit(solution)/shard_map/all_to_all | solution.py:180
  30.5 0.4 average_and_quantize.1
  30.9 10.3 %all_to_all.22 = f16[8,56,128]{2,1,0:T(8,128)(2,1)S(1)} all-to-all(f16[8,56,128]{2,1,0:T(8,128)(2,1)S(1)} %bitcast.43), channel_id=1, replica_groups={{0,8,16,24,32,40,48,56},{64,72,80,88,96,104,112,120},{128,136,144,152,1..., dimensions={0} | all-to-all | bytes 229376 | tf_op jit(solution)/shard_map/all_to_all | solution.py:180
  41.2 0.0 copy-start.1
  41.2 0.2 grad_and_squares.1
  41.4 14.6 %all_to_all.23 = f32[8,1,128]{2,1,0:T(1,128)S(1)} all-to-all(f32[8,1,128]{2,1,0:T(1,128)S(1)} %bitcast.41), channel_id=1, replica_groups={{0,33,2,35,4,37,6,39},{8,41,10,43,12,45,14,47},{16,49,18,51,20,53,22,55..., dimensions={0} | all-to-all | bytes 8192 | tf_op jit(solution)/shard_map/all_to_all | solution.py:197
  56.0 0.0 copy-done.1
  56.0 0.8 %update.1 = (f32[448,128]{1,0:T(8,128)}, f32[448,128]{1,0:T(8,128)}) custom-call(f32[448,128]{1,0:T(8,128)S(1)} %get-tuple-element.6.refs_0_, f32[448,128]{1,0:T(8,128)S(1)} %bitcast.37, f32[448,128]{1,0:T(8,128)S(1)} %bitcast.39, f32[8,128]{1,0:T(8,128)S(1)} %bitcast.40), custom_call_target="tpu_custom_call" | custom-call | tf_op jit(solution)/shard_map/update/pallas_call | solution.py:168
  (4 shorter events, 0.1 us)
Async XLA Ops:
  0.6 16.0 %copy-start = (f32[4,14336]{1,0:T(4,128)S(1)}, f32[4,14336]{1,0:T(4,128)}, u32[]{:S(2)}) copy-start(f32[4,14336]{1,0:T(4,128)} %param.4) | copy-start | bytes 688132
  41.2 14.9 %copy-start.1 = (f32[4,14336]{1,0:T(4,128)S(1)}, f32[4,14336]{1,0:T(4,128)}, u32[]{:S(2)}) copy-start(f32[4,14336]{1,0:T(4,128)} %param.5) | copy-start | bytes 688132

commit v8 on v7

--- a/solution.py
+++ b/solution.py
@@ -102,11 +102,15 @@
     return jnp.maximum(top, jnp.where(lane < 16, pltpu.roll(top, LANES - 16, 1), pltpu.roll(top, 16, 1)))
 
 
+def place_in_cell(rep):
+    return lax.rem(rep // 8, 2) * 4 + lax.rem(rep // 2, 2) * 2 + lax.rem(rep, 2)
+
+
 def first_kernel(local_ref, base_ref, out_ref):
     rows = base_ref.shape[0] // UNIT
     ones = block_ones()
     lane = index_of((UNIT, LANES), 1) % QBLOCK
-    mine = lax.rem(lax.axis_index("rep"), UNIT)
+    mine = place_in_cell(lax.axis_index("rep"))
     base = base_ref[pl.ds(pl.multiple_of(mine * rows, UNIT), rows)]
     local = local_ref[...].astype(jnp.float32)
     starts = range(0, rows, UNIT)
@@ -173,8 +177,7 @@
     shards = lax.axis_size("fsdp")
     rows, width = base.shape
     units = rows * width // LANES
-    planes = [[y * UNIT + q for q in range(UNIT)] for y in range(replicas // UNIT)]
-    lines = [[y * UNIT + q for y in range(replicas // UNIT)] for q in range(UNIT)]
+    cells, across = cell_groups()
 
     def exchange(array, peers):
         return lax.all_to_all(array, "rep", split_axis=0, concat_axis=0, tiled=True, axis_index_groups=peers)
@@ -188,11 +191,11 @@
 
     base_units = to_units(base)
     local = local_params[0].reshape(rows, width // LANES, LANES).transpose(1, 0, 2)
-    local = exchange(local, planes).reshape(units, LANES)
+    local = exchange(local, cells).reshape(units, LANES)
     sums = call(first_kernel, "quantize_and_add", shape(units), local, base_units)
-    sums = exchange_roots(sums, lines)
+    sums = exchange_roots(sums, across)
     parts = call(lambda *refs: second_kernel(*refs, replicas=replicas), "average_and_quantize", shape(units), sums)
-    parts = exchange_roots(parts, planes)
+    parts = exchange_roots(parts, cells)
     grad, squares = call(third_kernel, "grad_and_squares", (shape(units), shape(shards)), parts)
     squares = lax.all_to_all(
         squares.reshape(shards, 1, LANES), ("rep", "fsdp"), split_axis=0, concat_axis=0, tiled=True, axis_index_groups=groups
@@ -210,6 +213,15 @@
     return from_units(new_base, rows, width), from_units(new_momentum, rows, width)
 
 
+def cell_groups():
+    cells = [
+        [((2 * y + a) * 4 + 2 * z + b) * 2 + core for a in range(2) for b in range(2) for core in range(2)]
+        for y in range(4)
+        for z in range(2)
+    ]
+    return cells, [list(group) for group in zip(*cells)]
+
+
 def near_groups(mesh):
     replicas, shards = mesh.shape["rep"], mesh.shape["fsdp"]
 

time: 57.2 us -> 56.4 us (0.986)
  blocking collectives: 54 us -> 53.1 us
    all_to_all x3, blocking collectives: 39.3 us -> 37.2 us  [exchange(): lax.all_to_all(array, 'rep', split_axis=0, concat_axis=0, tiled=True, axi...]
    all_to_all x1, blocking collectives: 14.6 us -> 15.9 us  [per_device(): lax.all_to_all(squares.reshape(shards, 1, LANES), ('rep', 'fsdp'), split_...]
where the time goes in v8:
time: 56.4 us; the launch traced here: 56 us
  blocking collectives  53.1 us (94%)
  Pallas kernels  2.13 us (4%)
  between operations  0.69 us (1%)
    all_to_all x3, blocking collectives, exchange(): lax.all_to_all(array, 'rep', split_axis=0, concat_axis=0, tiled=True, axi...  37.2 us
    all_to_all x1, blocking collectives, per_device(): lax.all_to_all(squares.reshape(shards, 1, LANES), ('rep', 'fsdp'), split_...  15.9 us
    pallas_call x4, Pallas kernels, call(): pl.pallas_call(kernel, name=name, compiler_params=PARAMS, out_shape=out_s...  2.13 us

profile of v8, /device:TPU:1, one launch (start us, length us, event | category | flops | bytes accessed | tf_op | source)
XLA Modules:
  0.0 56.0 jit_solution(3058972586227576468)
XLA Ops:
  0.6 0.0 copy-start
  0.6 14.5 %all_to_all.20 = bf16[112,4,128]{2,1,0:T(4,128)(2,1)S(1)} all-to-all(bf16[112,4,128]{2,1,0:T(4,128)(2,1)} %bitcast.44), channel_id=1, replica_groups={{0,8,16,24,64,72,80,88},{32,40,48,56,96,104,112,120},{128,136,144,152,1..., dimensions={0} | all-to-all | bytes 229376 | tf_op jit(solution)/shard_map/all_to_all | solution.py:183
  15.1 0.0 copy-done
  15.1 0.7 %quantize_and_add.1 = f32[448,128]{1,0:T(8,128)S(1)} custom-call(bf16[448,128]{1,0:T(8,128)(2,1)S(1)} %bitcast.38, f32[448,128]{1,0:T(8,128)S(1)} %bitcast.36), custom_call_target="tpu_custom_call" | custom-call | tf_op jit(solution)/shard_map/quantize_and_add/pallas_call | solution.py:172
  15.9 13.8 %all_to_all.21 = f16[8,56,128]{2,1,0:T(8,128)(2,1)S(1)} all-to-all(f16[8,56,128]{2,1,0:T(8,128)(2,1)S(1)} %bitcast.42), channel_id=1, replica_groups={{0,32,128,160,256,288,384,416},{8,40,136,168,264,296,392,424},{16,48,14..., dimensions={0} | all-to-all | bytes 229376 | tf_op jit(solution)/shard_map/all_to_all | solution.py:183
  29.8 0.4 average_and_quantize.1
  30.2 8.9 %all_to_all.22 = f16[8,56,128]{2,1,0:T(8,128)(2,1)S(1)} all-to-all(f16[8,56,128]{2,1,0:T(8,128)(2,1)S(1)} %bitcast.43), channel_id=1, replica_groups={{0,8,16,24,64,72,80,88},{32,40,48,56,96,104,112,120},{128,136,144,152,1..., dimensions={0} | all-to-all | bytes 229376 | tf_op jit(solution)/shard_map/all_to_all | solution.py:183
  39.0 0.0 copy-start.1
  39.0 0.2 grad_and_squares.1
  39.3 15.9 %all_to_all.23 = f32[8,1,128]{2,1,0:T(1,128)S(1)} all-to-all(f32[8,1,128]{2,1,0:T(1,128)S(1)} %bitcast.41), channel_id=1, replica_groups={{0,33,2,35,4,37,6,39},{8,41,10,43,12,45,14,47},{16,49,18,51,20,53,22,55..., dimensions={0} | all-to-all | bytes 8192 | tf_op jit(solution)/shard_map/all_to_all | solution.py:200
  55.2 0.0 copy-done.1
  55.2 0.8 %update.1 = (f32[448,128]{1,0:T(8,128)}, f32[448,128]{1,0:T(8,128)}) custom-call(f32[448,128]{1,0:T(8,128)S(1)} %get-tuple-element.6.refs_0_, f32[448,128]{1,0:T(8,128)S(1)} %bitcast.37, f32[448,128]{1,0:T(8,128)S(1)} %bitcast.39, f32[8,128]{1,0:T(8,128)S(1)} %bitcast.40), custom_call_target="tpu_custom_call" | custom-call | tf_op jit(solution)/shard_map/update/pallas_call | solution.py:172
  (4 shorter events, 0.1 us)
Async XLA Ops:
  0.6 14.5 %copy-start = (f32[4,14336]{1,0:T(4,128)S(1)}, f32[4,14336]{1,0:T(4,128)}, u32[]{:S(2)}) copy-start(f32[4,14336]{1,0:T(4,128)} %param.4) | copy-start | bytes 688132
  39.0 16.2 %copy-start.1 = (f32[4,14336]{1,0:T(4,128)S(1)}, f32[4,14336]{1,0:T(4,128)}, u32[]{:S(2)}) copy-start(f32[4,14336]{1,0:T(4,128)} %param.5) | copy-start | bytes 688132

commit v9 on v8

--- a/solution.py
+++ b/solution.py
@@ -103,7 +103,7 @@
 
 
 def place_in_cell(rep):
-    return lax.rem(rep // 8, 2) * 4 + lax.rem(rep // 2, 2) * 2 + lax.rem(rep, 2)
+    return lax.rem(rep // 8 + rep // 32, 2) * 4 + lax.rem(rep // 2, 2) * 2 + lax.rem(rep, 2)
 
 
 def first_kernel(local_ref, base_ref, out_ref):
@@ -215,7 +215,7 @@
 
 def cell_groups():
     cells = [
-        [((2 * y + a) * 4 + 2 * z + b) * 2 + core for a in range(2) for b in range(2) for core in range(2)]
+        [((2 * y + (a + y // 2) % 2) * 4 + 2 * z + b) * 2 + core for a in range(2) for b in range(2) for core in range(2)]
         for y in range(4)
         for z in range(2)
     ]

time: 56.4 us -> 55.4 us (0.982)
  blocking collectives: 53.1 us -> 52.1 us
    all_to_all x3, blocking collectives: 37.2 us -> 36.3 us  [exchange(): lax.all_to_all(array, 'rep', split_axis=0, concat_axis=0, tiled=True, axi...]
where the time goes in v9:
time: 55.4 us; the launch traced here: 55 us
  blocking collectives  52.1 us (94%)
  Pallas kernels  2.13 us (4%)
  between operations  0.69 us (1%)
    all_to_all x3, blocking collectives, exchange(): lax.all_to_all(array, 'rep', split_axis=0, concat_axis=0, tiled=True, axi...  36.3 us
    all_to_all x1, blocking collectives, per_device(): lax.all_to_all(squares.reshape(shards, 1, LANES), ('rep', 'fsdp'), split_...  15.8 us
    pallas_call x4, Pallas kernels, call(): pl.pallas_call(kernel, name=name, compiler_params=PARAMS, out_shape=out_s...  2.13 us

profile of v9, /device:TPU:1, one launch (start us, length us, event | category | flops | bytes accessed | tf_op | source)
XLA Modules:
  0.0 55.0 jit_solution(12722916379976670663)
XLA Ops:
  0.6 0.0 copy-start
  0.6 14.5 %all_to_all.20 = bf16[112,4,128]{2,1,0:T(4,128)(2,1)S(1)} all-to-all(bf16[112,4,128]{2,1,0:T(4,128)(2,1)} %bitcast.44), channel_id=1, replica_groups={{0,8,16,24,64,72,80,88},{32,40,48,56,96,104,112,120},{128,136,144,152,1..., dimensions={0} | all-to-all | bytes 229376 | tf_op jit(solution)/shard_map/all_to_all | solution.py:183
  15.1 0.0 copy-done
  15.1 0.7 %quantize_and_add.1 = f32[448,128]{1,0:T(8,128)S(1)} custom-call(bf16[448,128]{1,0:T(8,128)(2,1)S(1)} %bitcast.38, f32[448,128]{1,0:T(8,128)S(1)} %bitcast.36), custom_call_target="tpu_custom_call" | custom-call | tf_op jit(solution)/shard_map/quantize_and_add/pallas_call | solution.py:172
  15.9 12.8 %all_to_all.21 = f16[8,56,128]{2,1,0:T(8,128)(2,1)S(1)} all-to-all(f16[8,56,128]{2,1,0:T(8,128)(2,1)S(1)} %bitcast.42), channel_id=1, replica_groups={{0,32,128,160,320,352,448,480},{8,40,136,168,328,360,456,488},{16,48,14..., dimensions={0} | all-to-all | bytes 229376 | tf_op jit(solution)/shard_map/all_to_all | solution.py:183
  28.7 0.4 average_and_quantize.1
  29.1 9.0 %all_to_all.22 = f16[8,56,128]{2,1,0:T(8,128)(2,1)S(1)} all-to-all(f16[8,56,128]{2,1,0:T(8,128)(2,1)S(1)} %bitcast.43), channel_id=1, replica_groups={{0,8,16,24,64,72,80,88},{32,40,48,56,96,104,112,120},{128,136,144,152,1..., dimensions={0} | all-to-all | bytes 229376 | tf_op jit(solution)/shard_map/all_to_all | solution.py:183
  38.1 0.0 copy-start.1
  38.2 0.2 grad_and_squares.1
  38.4 15.8 %all_to_all.23 = f32[8,1,128]{2,1,0:T(1,128)S(1)} all-to-all(f32[8,1,128]{2,1,0:T(1,128)S(1)} %bitcast.41), channel_id=1, replica_groups={{0,33,2,35,4,37,6,39},{8,41,10,43,12,45,14,47},{16,49,18,51,20,53,22,55..., dimensions={0} | all-to-all | bytes 8192 | tf_op jit(solution)/shard_map/all_to_all | solution.py:200
  54.2 0.0 copy-done.1
  54.2 0.8 %update.1 = (f32[448,128]{1,0:T(8,128)}, f32[448,128]{1,0:T(8,128)}) custom-call(f32[448,128]{1,0:T(8,128)S(1)} %get-tuple-element.6.refs_0_, f32[448,128]{1,0:T(8,128)S(1)} %bitcast.37, f32[448,128]{1,0:T(8,128)S(1)} %bitcast.39, f32[8,128]{1,0:T(8,128)S(1)} %bitcast.40), custom_call_target="tpu_custom_call" | custom-call | tf_op jit(solution)/shard_map/update/pallas_call | solution.py:172
  (4 shorter events, 0.1 us)
Async XLA Ops:
  0.6 14.5 %copy-start = (f32[4,14336]{1,0:T(4,128)S(1)}, f32[4,14336]{1,0:T(4,128)}, u32[]{:S(2)}) copy-start(f32[4,14336]{1,0:T(4,128)} %param.4) | copy-start | bytes 688132
  38.1 16.1 %copy-start.1 = (f32[4,14336]{1,0:T(4,128)S(1)}, f32[4,14336]{1,0:T(4,128)}, u32[]{:S(2)}) copy-start(f32[4,14336]{1,0:T(4,128)} %param.5) | copy-start | bytes 688132

commit v10 on v9

--- a/solution.py
+++ b/solution.py
@@ -69,20 +69,30 @@
     return jnp.dot(values.astype(jnp.bfloat16), ones, preferred_element_type=jnp.float32)
 
 
+def merged_four(arrays, lane, unit):
+    merged = None
+    for k, array in enumerate(arrays):
+        place = 3 - (k % 2 * 2 + k // 2)
+        top = array
+        for other in range(4):
+            if other != place:
+                top = jnp.maximum(top, pltpu.roll(array, (place - other) * unit % LANES, 1))
+        merged = top if merged is None else jnp.where(lane // unit % 4 == place, top, merged)
+    return merged
+
+
 def packed_top(arrays, lane):
     arrays = [jnp.abs(array) for array in arrays]
-    shift = QBLOCK // 2
-    while shift:
-        if len(arrays) % 2:
-            arrays.append(jnp.zeros_like(arrays[0]))
-        halves = []
-        for one, two in zip(arrays[::2], arrays[1::2]):
-            one = jnp.maximum(one, pltpu.roll(one, shift, 1))
-            two = jnp.maximum(two, pltpu.roll(two, LANES - shift, 1))
-            halves.append(jnp.where(lane & shift != 0, one, two))
-        arrays = halves
-        shift //= 2
-    return arrays[0]
+    arrays += [jnp.zeros_like(arrays[0])] * (-len(arrays) % 8)
+    half = QBLOCK // 2
+    halves = []
+    for one, two in zip(arrays[::2], arrays[1::2]):
+        one = jnp.maximum(one, pltpu.roll(one, half, 1))
+        two = jnp.maximum(two, pltpu.roll(two, LANES - half, 1))
+        halves.append(jnp.where(lane >= half, one, two))
+    arrays = [merged_four(halves[k : k + 4], lane, 4) for k in range(0, len(halves), 4)]
+    arrays += [jnp.zeros_like(arrays[0])] * (4 - len(arrays))
+    return merged_four(arrays, lane, 1)
 
 
 def place_of(j):
@@ -103,7 +113,7 @@
 
 
 def place_in_cell(rep):
-    return lax.rem(rep // 8 + rep // 32, 2) * 4 + lax.rem(rep // 2, 2) * 2 + lax.rem(rep, 2)
+    return lax.rem(rep // 8 + rep // 32, 2) * 4 + lax.rem(rep // 2, 2) * 2 + lax.rem(rep + rep // 4, 2)
 
 
 def first_kernel(local_ref, base_ref, out_ref):
@@ -122,10 +132,11 @@
         scales += [jnp.where(lane == place_of(j), scale, 0.0) for j in range(len(group))]
     total = jnp.zeros((rows, LANES), jnp.float32)
     count = len(starts)
-    for j in range(UNIT):
-        here = slice(j * count, (j + 1) * count)
-        scale = spread(jnp.concatenate(scales[here], axis=0), ones)
-        total += code_of(jnp.concatenate(deltas[here], axis=0), scale) * scale
+    scale = spread(jnp.concatenate(scales, axis=0), ones)
+    value = code_of(jnp.concatenate(deltas, axis=0), scale) * scale
+    total = value[:rows]
+    for j in range(1, UNIT):
+        total += value[j * rows : (j + 1) * rows]
     total = to_root(total, SUM_FACTOR)
     for j in range(UNIT):
         out_ref[j * rows : (j + 1) * rows] = total
@@ -143,17 +154,16 @@
         out_ref[j * rows : (j + 1) * rows] = message
 
 
-def third_kernel(in_ref, grad_ref, squares_ref):
+def third_kernel(in_ref, squares_ref):
     grad = from_root(in_ref[...], GRAD_FACTOR)
-    grad_ref[...] = grad
     total = jnp.sum((grad * grad).reshape(-1, UNIT, LANES), axis=0)
-    squares_ref[...] = jnp.full((UNIT, LANES), jnp.sum(total), jnp.float32)
-
-
-def fourth_kernel(grad_ref, base_ref, momentum_ref, squares_ref, new_base_ref, new_momentum_ref, *, limit):
-    squares = jnp.sum(squares_ref[...], axis=0, keepdims=True)
+    squares_ref[...] = jnp.broadcast_to(jnp.sum(total, axis=0, keepdims=True), (UNIT, LANES))
+
+
+def fourth_kernel(parts_ref, base_ref, momentum_ref, squares_ref, new_base_ref, new_momentum_ref, *, limit):
+    squares = jnp.sum(jnp.sum(squares_ref[...], axis=0, keepdims=True), axis=1, keepdims=True)
     factor = limit / jnp.maximum(jnp.sqrt(squares), limit)
-    scaled = factor * grad_ref[...]
+    scaled = factor * from_root(parts_ref[...], GRAD_FACTOR)
     momentum = decay * momentum_ref[...] + scaled
     new_momentum_ref[...] = momentum
     new_base_ref[...] = base_ref[...] - outer_rate * (scaled + decay * momentum)
@@ -196,7 +206,7 @@
     sums = exchange_roots(sums, across)
     parts = call(lambda *refs: second_kernel(*refs, replicas=replicas), "average_and_quantize", shape(units), sums)
     parts = exchange_roots(parts, cells)
-    grad, squares = call(third_kernel, "grad_and_squares", (shape(units), shape(shards)), parts)
+    squares = call(third_kernel, "add_squares", shape(shards), parts)
     squares = lax.all_to_all(
         squares.reshape(shards, 1, LANES), ("rep", "fsdp"), split_axis=0, concat_axis=0, tiled=True, axis_index_groups=groups
     ).reshape(shards, LANES)
@@ -205,7 +215,7 @@
         lambda *refs: fourth_kernel(*refs, limit=limit),
         "update",
         (shape(units), shape(units)),
-        grad,
+        parts,
         base_units,
         to_units(momentum),
         squares,
@@ -215,7 +225,7 @@
 
 def cell_groups():
     cells = [
-        [((2 * y + (a + y // 2) % 2) * 4 + 2 * z + b) * 2 + core for a in range(2) for b in range(2) for core in range(2)]
+        [((2 * y + (a + y // 2) % 2) * 4 + 2 * z + b) * 2 + (core + z) % 2 for a in range(2) for b in range(2) for core in range(2)]
         for y in range(4)
         for z in range(2)
     ]

time: 55.4 us -> 55.2 us (level)
    all_to_all x1, blocking collectives: 15.8 us -> 16.7 us  [per_device(): lax.all_to_all(squares.reshape(shards, 1, LANES), ('rep', 'fsdp'), split_...]
    all_to_all x3, blocking collectives: 36.3 us -> 35.5 us  [exchange(): lax.all_to_all(array, 'rep', split_axis=0, concat_axis=0, tiled=True, axi...]
where the time goes in v10:
time: 55.2 us; the launch traced here: 54.9 us
  blocking collectives  52.1 us (94%)
  Pallas kernels  1.95 us (4%)
  between operations  0.68 us (1%)
    all_to_all x3, blocking collectives, exchange(): lax.all_to_all(array, 'rep', split_axis=0, concat_axis=0, tiled=True, axi...  35.5 us
    all_to_all x1, blocking collectives, per_device(): lax.all_to_all(squares.reshape(shards, 1, LANES), ('rep', 'fsdp'), split_...  16.7 us
    pallas_call x4, Pallas kernels, call(): pl.pallas_call(kernel, name=name, compiler_params=PARAMS, out_shape=out_s...  1.95 us

profile of v10, /device:TPU:1, one launch (start us, length us, event | category | flops | bytes accessed | tf_op | source)
XLA Modules:
  0.0 54.9 jit_solution(15844235259865005461)
XLA Ops:
  0.6 0.0 copy-start
  0.6 14.5 %all_to_all.20 = bf16[112,4,128]{2,1,0:T(4,128)(2,1)S(1)} all-to-all(bf16[112,4,128]{2,1,0:T(4,128)(2,1)} %bitcast.44), channel_id=1, replica_groups={{0,8,16,24,64,72,80,88},{40,32,56,48,104,96,120,112},{128,136,144,152,1..., dimensions={0} | all-to-all | bytes 229376 | tf_op jit(solution)/shard_map/all_to_all | solution.py:193
  15.1 0.0 copy-done
  15.1 0.6 %quantize_and_add.1 = f32[448,128]{1,0:T(8,128)S(1)} custom-call(bf16[448,128]{1,0:T(8,128)(2,1)S(1)} %bitcast.38, f32[448,128]{1,0:T(8,128)S(1)} %bitcast.36), custom_call_target="tpu_custom_call" | custom-call | tf_op jit(solution)/shard_map/quantize_and_add/pallas_call | solution.py:182
  15.8 14.4 %all_to_all.21 = f16[8,56,128]{2,1,0:T(8,128)(2,1)S(1)} all-to-all(f16[8,56,128]{2,1,0:T(8,128)(2,1)S(1)} %bitcast.42), channel_id=1, replica_groups={{0,40,128,168,320,360,448,488},{8,32,136,160,328,352,456,480},{16,56,14..., dimensions={0} | all-to-all | bytes 229376 | tf_op jit(solution)/shard_map/all_to_all | solution.py:193
  30.2 0.4 average_and_quantize.1
  30.6 6.6 %all_to_all.22 = f16[8,56,128]{2,1,0:T(8,128)(2,1)S(1)} all-to-all(f16[8,56,128]{2,1,0:T(8,128)(2,1)S(1)} %bitcast.43), channel_id=1, replica_groups={{0,8,16,24,64,72,80,88},{40,32,56,48,104,96,120,112},{128,136,144,152,1..., dimensions={0} | all-to-all | bytes 229376 | tf_op jit(solution)/shard_map/all_to_all | solution.py:193
  37.2 0.0 copy-start.1
  37.2 0.1 add_squares.1
  37.3 16.7 %all_to_all.23 = f32[8,1,128]{2,1,0:T(1,128)S(1)} all-to-all(f32[8,1,128]{2,1,0:T(1,128)S(1)} %bitcast.41), channel_id=1, replica_groups={{0,33,2,35,4,37,6,39},{8,41,10,43,12,45,14,47},{16,49,18,51,20,53,22,55..., dimensions={0} | all-to-all | bytes 8192 | tf_op jit(solution)/shard_map/all_to_all | solution.py:210
  53.9 0.0 copy-done.1
  53.9 0.9 %update.1 = (f32[448,128]{1,0:T(8,128)}, f32[448,128]{1,0:T(8,128)}) custom-call(f32[448,128]{1,0:T(8,128)S(1)} %bitcast_convert_fusion.1.in_ref.refs_0_, f32[448,128]{1,0:T(8,128)S(1)} %bitcast.37, f32[448,128]{1,0:T(8,128)S(1)} %bitcast.39, f32[8,128]{1,0:T(8,128)S(1)} %bitcast.40), custom_call_target="tpu_custom_call" | custom-call | tf_op jit(solution)/shard_map/update/pallas_call | solution.py:182
  (4 shorter events, 0.1 us)
Async XLA Ops:
  0.6 14.5 %copy-start = (f32[4,14336]{1,0:T(4,128)S(1)}, f32[4,14336]{1,0:T(4,128)}, u32[]{:S(2)}) copy-start(f32[4,14336]{1,0:T(4,128)} %param.4) | copy-start | bytes 688132
  37.2 16.8 %copy-start.1 = (f32[4,14336]{1,0:T(4,128)S(1)}, f32[4,14336]{1,0:T(4,128)}, u32[]{:S(2)}) copy-start(f32[4,14336]{1,0:T(4,128)} %param.5) | copy-start | bytes 688132

commit v11 on v10

--- a/solution.py
+++ b/solution.py
@@ -113,7 +113,9 @@
 
 
 def place_in_cell(rep):
-    return lax.rem(rep // 8 + rep // 32, 2) * 4 + lax.rem(rep // 2, 2) * 2 + lax.rem(rep + rep // 4, 2)
+    rep = lax.rem(rep + 8, 64)
+    y, z = rep // 16, lax.rem(rep // 4, 2)
+    return lax.rem(rep // 8 + (y + 1) // 2, 2) * 4 + lax.rem(rep // 2, 2) * 2 + lax.rem(rep + z, 2)
 
 
 def first_kernel(local_ref, base_ref, out_ref):
@@ -225,7 +227,7 @@
 
 def cell_groups():
     cells = [
-        [((2 * y + (a + y // 2) % 2) * 4 + 2 * z + b) * 2 + (core + z) % 2 for a in range(2) for b in range(2) for core in range(2)]
+        [((2 * y + (a + (y + 1) // 2) % 2 + 7) % 8 * 4 + 2 * z + b) * 2 + (core + z) % 2 for a in range(2) for b in range(2) for core in range(2)]
         for y in range(4)
         for z in range(2)
     ]
@@ -240,7 +242,7 @@
 
     partner = {0: 6, 1: 7, 2: 4, 3: 5}
     return [
-        [index(y, z, core, x) for x in range(shards // 2) for z in (low, partner[low])]
+        [index(y, z, core, x) for x in range(shards // 2) for z in (low, 7 - low if core else partner[low])]
         for y in range(replicas // 8)
         for low in range(4)
         for core in range(2)

time: 55.2 us -> 53.8 us (0.975)
  the two profiles are of different devices: /device:TPU:1 before, /device:TPU:8 now
where the time goes in v11:
time: 53.8 us; the launch traced here: 53.5 us
  blocking collectives  50.8 us (94%)
  Pallas kernels  1.95 us (4%)
  between operations  0.68 us (1%)
    all_to_all x3, blocking collectives, exchange(): lax.all_to_all(array, 'rep', split_axis=0, concat_axis=0, tiled=True, axi...  33.8 us
    all_to_all x1, blocking collectives, per_device(): lax.all_to_all(squares.reshape(shards, 1, LANES), ('rep', 'fsdp'), split_...  17 us
    pallas_call x4, Pallas kernels, call(): pl.pallas_call(kernel, name=name, compiler_params=PARAMS, out_shape=out_s...  1.95 us

profile of v11, /device:TPU:8, one launch (start us, length us, event | category | flops | bytes accessed | tf_op | source)
XLA Modules:
  0.0 53.5 jit_solution(16060789698875387572)
XLA Ops:
  0.6 0.0 copy-start
  0.6 9.3 %all_to_all.20 = bf16[112,4,128]{2,1,0:T(4,128)(2,1)S(1)} all-to-all(bf16[112,4,128]{2,1,0:T(4,128)(2,1)} %bitcast.44), channel_id=1, replica_groups={{448,456,464,472,0,8,16,24},{488,480,504,496,40,32,56,48},{128,136,144,..., dimensions={0} | all-to-all | bytes 229376 | tf_op jit(solution)/shard_map/all_to_all | solution.py:195
  9.9 0.0 copy-done
  9.9 0.6 %quantize_and_add.1 = f32[448,128]{1,0:T(8,128)S(1)} custom-call(bf16[448,128]{1,0:T(8,128)(2,1)S(1)} %bitcast.38, f32[448,128]{1,0:T(8,128)S(1)} %bitcast.36), custom_call_target="tpu_custom_call" | custom-call | tf_op jit(solution)/shard_map/quantize_and_add/pallas_call | solution.py:184
  10.5 16.1 %all_to_all.21 = f16[8,56,128]{2,1,0:T(8,128)(2,1)S(1)} all-to-all(f16[8,56,128]{2,1,0:T(8,128)(2,1)S(1)} %bitcast.42), channel_id=1, replica_groups={{448,488,128,168,256,296,320,360},{456,480,136,160,264,288,328,352},{46..., dimensions={0} | all-to-all | bytes 229376 | tf_op jit(solution)/shard_map/all_to_all | solution.py:195
  26.7 0.4 average_and_quantize.1
  27.1 8.4 %all_to_all.22 = f16[8,56,128]{2,1,0:T(8,128)(2,1)S(1)} all-to-all(f16[8,56,128]{2,1,0:T(8,128)(2,1)S(1)} %bitcast.43), channel_id=1, replica_groups={{448,456,464,472,0,8,16,24},{488,480,504,496,40,32,56,48},{128,136,144,..., dimensions={0} | all-to-all | bytes 229376 | tf_op jit(solution)/shard_map/all_to_all | solution.py:195
  35.5 0.0 copy-start.1
  35.5 0.1 add_squares.1
  35.6 17.0 %all_to_all.23 = f32[8,1,128]{2,1,0:T(1,128)S(1)} all-to-all(f32[8,1,128]{2,1,0:T(1,128)S(1)} %bitcast.41), channel_id=1, replica_groups={{0,33,2,35,4,37,6,39},{8,57,10,59,12,61,14,63},{16,49,18,51,20,53,22,55..., dimensions={0} | all-to-all | bytes 8192 | tf_op jit(solution)/shard_map/all_to_all | solution.py:212
  52.6 0.0 copy-done.1
  52.6 0.9 %update.1 = (f32[448,128]{1,0:T(8,128)}, f32[448,128]{1,0:T(8,128)}) custom-call(f32[448,128]{1,0:T(8,128)S(1)} %bitcast_convert_fusion.1.in_ref.refs_0_, f32[448,128]{1,0:T(8,128)S(1)} %bitcast.37, f32[448,128]{1,0:T(8,128)S(1)} %bitcast.39, f32[8,128]{1,0:T(8,128)S(1)} %bitcast.40), custom_call_target="tpu_custom_call" | custom-call | tf_op jit(solution)/shard_map/update/pallas_call | solution.py:184
  (4 shorter events, 0.1 us)
Async XLA Ops:
  0.6 9.3 %copy-start = (f32[4,14336]{1,0:T(4,128)S(1)}, f32[4,14336]{1,0:T(4,128)}, u32[]{:S(2)}) copy-start(f32[4,14336]{1,0:T(4,128)} %param.4) | copy-start | bytes 688132
  35.5 17.1 %copy-start.1 = (f32[4,14336]{1,0:T(4,128)S(1)}, f32[4,14336]{1,0:T(4,128)}, u32[]{:S(2)}) copy-start(f32[4,14336]{1,0:T(4,128)} %param.5) | copy-start | bytes 688132

commit v12 on v11

--- a/solution.py
+++ b/solution.py
@@ -231,7 +231,8 @@
         for y in range(4)
         for z in range(2)
     ]
-    return cells, [list(group) for group in zip(*cells)]
+    order = sorted(range(8), key=lambda k: (k // 2 != 2, k % 2 == 0, k))
+    return cells, [[group[k] for k in order] for group in zip(*cells)]
 
 
 def near_groups(mesh):
@@ -242,7 +243,7 @@
 
     partner = {0: 6, 1: 7, 2: 4, 3: 5}
     return [
-        [index(y, z, core, x) for x in range(shards // 2) for z in (low, 7 - low if core else partner[low])]
+        [index(y, z, core, x) for x in range(shards // 2) for z in (low, 7 - low if core else partner[low])][::-1]
         for y in range(replicas // 8)
         for low in range(4)
         for core in range(2)

time: 53.8 us -> 49.7 us (0.924)
  the two profiles are of different devices: /device:TPU:8 before, /device:TPU:1 now
where the time goes in v12:
time: 49.7 us; the launch traced here: 49.2 us
  blocking collectives  46.5 us (94%)
  Pallas kernels  1.95 us (4%)
  between operations  0.68 us (1%)
    all_to_all x3, blocking collectives, exchange(): lax.all_to_all(array, 'rep', split_axis=0, concat_axis=0, tiled=True, axi...  35.4 us
    all_to_all x1, blocking collectives, per_device(): lax.all_to_all(squares.reshape(shards, 1, LANES), ('rep', 'fsdp'), split_...  11.1 us
    pallas_call x4, Pallas kernels, call(): pl.pallas_call(kernel, name=name, compiler_params=PARAMS, out_shape=out_s...  1.95 us

profile of v12, /device:TPU:1, one launch (start us, length us, event | category | flops | bytes accessed | tf_op | source)
XLA Modules:
  0.0 49.2 jit_solution(6562326996587150896)
XLA Ops:
  0.6 0.0 copy-start
  0.6 14.8 %all_to_all.20 = bf16[112,4,128]{2,1,0:T(4,128)(2,1)S(1)} all-to-all(bf16[112,4,128]{2,1,0:T(4,128)(2,1)} %bitcast.44), channel_id=1, replica_groups={{448,456,464,472,0,8,16,24},{488,480,504,496,40,32,56,48},{128,136,144,..., dimensions={0} | all-to-all | bytes 229376 | tf_op jit(solution)/shard_map/all_to_all | solution.py:195
  15.4 0.0 copy-done
  15.4 0.6 %quantize_and_add.1 = f32[448,128]{1,0:T(8,128)S(1)} custom-call(bf16[448,128]{1,0:T(8,128)(2,1)S(1)} %bitcast.38, f32[448,128]{1,0:T(8,128)S(1)} %bitcast.36), custom_call_target="tpu_custom_call" | custom-call | tf_op jit(solution)/shard_map/quantize_and_add/pallas_call | solution.py:184
  16.0 12.4 %all_to_all.21 = f16[8,56,128]{2,1,0:T(8,128)(2,1)S(1)} all-to-all(f16[8,56,128]{2,1,0:T(8,128)(2,1)S(1)} %bitcast.42), channel_id=1, replica_groups={{296,256,488,168,360,448,128,320},{288,264,480,160,352,456,136,328},{31..., dimensions={0} | all-to-all | bytes 229376 | tf_op jit(solution)/shard_map/all_to_all | solution.py:195
  28.5 0.4 average_and_quantize.1
  28.9 8.2 %all_to_all.22 = f16[8,56,128]{2,1,0:T(8,128)(2,1)S(1)} all-to-all(f16[8,56,128]{2,1,0:T(8,128)(2,1)S(1)} %bitcast.43), channel_id=1, replica_groups={{448,456,464,472,0,8,16,24},{488,480,504,496,40,32,56,48},{128,136,144,..., dimensions={0} | all-to-all | bytes 229376 | tf_op jit(solution)/shard_map/all_to_all | solution.py:195
  37.1 0.0 copy-start.1
  37.1 0.1 add_squares.1
  37.2 11.1 %all_to_all.23 = f32[8,1,128]{2,1,0:T(1,128)S(1)} all-to-all(f32[8,1,128]{2,1,0:T(1,128)S(1)} %bitcast.41), channel_id=1, replica_groups={{39,6,37,4,35,2,33,0},{63,14,61,12,59,10,57,8},{55,22,53,20,51,18,49,16..., dimensions={0} | all-to-all | bytes 8192 | tf_op jit(solution)/shard_map/all_to_all | solution.py:212
  48.3 0.0 copy-done.1
  48.3 0.9 %update.1 = (f32[448,128]{1,0:T(8,128)}, f32[448,128]{1,0:T(8,128)}) custom-call(f32[448,128]{1,0:T(8,128)S(1)} %bitcast_convert_fusion.1.in_ref.refs_0_, f32[448,128]{1,0:T(8,128)S(1)} %bitcast.37, f32[448,128]{1,0:T(8,128)S(1)} %bitcast.39, f32[8,128]{1,0:T(8,128)S(1)} %bitcast.40), custom_call_target="tpu_custom_call" | custom-call | tf_op jit(solution)/shard_map/update/pallas_call | solution.py:184
  (4 shorter events, 0.1 us)
Async XLA Ops:
  0.6 14.8 %copy-start = (f32[4,14336]{1,0:T(4,128)S(1)}, f32[4,14336]{1,0:T(4,128)}, u32[]{:S(2)}) copy-start(f32[4,14336]{1,0:T(4,128)} %param.4) | copy-start | bytes 688132
  37.1 11.2 %copy-start.1 = (f32[4,14336]{1,0:T(4,128)S(1)}, f32[4,14336]{1,0:T(4,128)}, u32[]{:S(2)}) copy-start(f32[4,14336]{1,0:T(4,128)} %param.5) | copy-start | bytes 688132

commit v13 on v12

--- a/solution.py
+++ b/solution.py
@@ -243,7 +243,7 @@
 
     partner = {0: 6, 1: 7, 2: 4, 3: 5}
     return [
-        [index(y, z, core, x) for x in range(shards // 2) for z in (low, 7 - low if core else partner[low])][::-1]
+        [index(y, z, core, x) for z in (low, 7 - low if core else partner[low]) for x in range(shards // 2)][::-1]
         for y in range(replicas // 8)
         for low in range(4)
         for core in range(2)

time: 49.7 us -> 49.7 us (level)
  no operation moved by 1% of the time
where the time goes in v13:
time: 49.7 us; the launch traced here: 49.2 us
  blocking collectives  46.5 us (94%)
  Pallas kernels  1.95 us (4%)
  between operations  0.68 us (1%)
    all_to_all x3, blocking collectives, exchange(): lax.all_to_all(array, 'rep', split_axis=0, concat_axis=0, tiled=True, axi...  35.4 us
    all_to_all x1, blocking collectives, per_device(): lax.all_to_all(squares.reshape(shards, 1, LANES), ('rep', 'fsdp'), split_...  11.1 us
    pallas_call x4, Pallas kernels, call(): pl.pallas_call(kernel, name=name, compiler_params=PARAMS, out_shape=out_s...  1.95 us

profile of v13, /device:TPU:1, one launch (start us, length us, event | category | flops | bytes accessed | tf_op | source)
XLA Modules:
  0.0 49.2 jit_solution(13579464221244506220)
XLA Ops:
  0.6 0.0 copy-start
  0.6 14.8 %all_to_all.20 = bf16[112,4,128]{2,1,0:T(4,128)(2,1)S(1)} all-to-all(bf16[112,4,128]{2,1,0:T(4,128)(2,1)} %bitcast.44), channel_id=1, replica_groups={{448,456,464,472,0,8,16,24},{488,480,504,496,40,32,56,48},{128,136,144,..., dimensions={0} | all-to-all | bytes 229376 | tf_op jit(solution)/shard_map/all_to_all | solution.py:195
  15.4 0.0 copy-done
  15.4 0.6 %quantize_and_add.1 = f32[448,128]{1,0:T(8,128)S(1)} custom-call(bf16[448,128]{1,0:T(8,128)(2,1)S(1)} %bitcast.38, f32[448,128]{1,0:T(8,128)S(1)} %bitcast.36), custom_call_target="tpu_custom_call" | custom-call | tf_op jit(solution)/shard_map/quantize_and_add/pallas_call | solution.py:184
  16.0 12.4 %all_to_all.21 = f16[8,56,128]{2,1,0:T(8,128)(2,1)S(1)} all-to-all(f16[8,56,128]{2,1,0:T(8,128)(2,1)S(1)} %bitcast.42), channel_id=1, replica_groups={{296,256,488,168,360,448,128,320},{288,264,480,160,352,456,136,328},{31..., dimensions={0} | all-to-all | bytes 229376 | tf_op jit(solution)/shard_map/all_to_all | solution.py:195
  28.5 0.4 average_and_quantize.1
  28.9 8.2 %all_to_all.22 = f16[8,56,128]{2,1,0:T(8,128)(2,1)S(1)} all-to-all(f16[8,56,128]{2,1,0:T(8,128)(2,1)S(1)} %bitcast.43), channel_id=1, replica_groups={{448,456,464,472,0,8,16,24},{488,480,504,496,40,32,56,48},{128,136,144,..., dimensions={0} | all-to-all | bytes 229376 | tf_op jit(solution)/shard_map/all_to_all | solution.py:195
  37.1 0.0 copy-start.1
  37.1 0.1 add_squares.1
  37.2 11.1 %all_to_all.23 = f32[8,1,128]{2,1,0:T(1,128)S(1)} all-to-all(f32[8,1,128]{2,1,0:T(1,128)S(1)} %bitcast.41), channel_id=1, replica_groups={{39,37,35,33,6,4,2,0},{63,61,59,57,14,12,10,8},{55,53,51,49,22,20,18,16..., dimensions={0} | all-to-all | bytes 8192 | tf_op jit(solution)/shard_map/all_to_all | solution.py:212
  48.3 0.0 copy-done.1
  48.3 0.9 %update.1 = (f32[448,128]{1,0:T(8,128)}, f32[448,128]{1,0:T(8,128)}) custom-call(f32[448,128]{1,0:T(8,128)S(1)} %bitcast_convert_fusion.1.in_ref.refs_0_, f32[448,128]{1,0:T(8,128)S(1)} %bitcast.37, f32[448,128]{1,0:T(8,128)S(1)} %bitcast.39, f32[8,128]{1,0:T(8,128)S(1)} %bitcast.40), custom_call_target="tpu_custom_call" | custom-call | tf_op jit(solution)/shard_map/update/pallas_call | solution.py:184
  (4 shorter events, 0.1 us)
Async XLA Ops:
  0.6 14.8 %copy-start = (f32[4,14336]{1,0:T(4,128)S(1)}, f32[4,14336]{1,0:T(4,128)}, u32[]{:S(2)}) copy-start(f32[4,14336]{1,0:T(4,128)} %param.4) | copy-start | bytes 688132
  37.1 11.2 %copy-start.1 = (f32[4,14336]{1,0:T(4,128)S(1)}, f32[4,14336]{1,0:T(4,128)}, u32[]{:S(2)}) copy-start(f32[4,14336]{1,0:T(4,128)} %param.5) | copy-start | bytes 688132
